TPU v7x, 32 devices: a whole 2x2x4 slice. The times are simulated.
32 devices in a mesh: img: 8 (over z, y), band: 4 (over x, core).
Axes of the slice: x: 2, y: 2, z: 4, core: 2. Of those that a mesh axis runs over, the one named last changes fastest.
Arguments:
- inputs: bfloat16 [256, 400, 432], P('img', 'band'), may hold values from -6 to 6
- cotangent: bfloat16 [256, 400, 432], P('img', 'band'), may hold values from -6 to 6
- grid_sizes: int32 [256], P('img'), may hold values from 10 to 18, as said below
- w_qkv: float32 [432, 1296], replicated, may hold values from -0.21875 to 0.21875
- w_out: float32 [432, 432], replicated, may hold values from -0.875 to 0.875
- w_fc1: float32 [432, 1728], replicated, may hold values from -0.3125 to 0.3125
- w_fc2: float32 [1728, 432], replicated, may hold values from -0.15625 to 0.15625
- norm_gains: float32 [2, 432], replicated, may hold values from 0.7 to 6.5
- biases: float32 [4, 432], replicated, may hold values from -1.75 to 1.75
- fc1_bias: float32 [1728], replicated, may hold values from -1.75 to 1.75
- head_params: float32 [4, 9], replicated, may hold values from -2 to 2, as said below
- rows_qkv: float32 [432], replicated, may hold values from 8.467612e-08 to 3.3424783e-07
- cols_qkv: float32 [1296], replicated, may hold values from 8.467612e-08 to 3.3424783e-07
- rows_out: float32 [432], replicated, may hold values from 8.484082e-09 to 3.3489798e-08
- cols_out: float32 [432], replicated, may hold values from 8.484082e-09 to 3.3489798e-08
- rows_fc1: float32 [432], replicated, may hold values from 1.8307755e-08 to 7.3677555e-08
- cols_fc1: float32 [1728], replicated, may hold values from 1.8307755e-08 to 7.3677555e-08
- rows_fc2: float32 [1728], replicated, may hold values from 8.467612e-08 to 3.3424783e-07
- cols_fc2: float32 [432], replicated, may hold values from 8.467612e-08 to 3.3424783e-07
- gain_moment: float32 [2, 432], replicated, may hold values from 5.8048983e-08 to 2.3219593e-07
- bias_moment: float32 [4, 432], replicated, may hold values from 3.3424783e-07 to 1.3369913e-06
- fc1_bias_moment: float32 [1728], replicated, may hold values from 1.2502857e-08 to 4.911837e-08
- head_moment: float32 [4, 9], replicated, may hold values from 3.3424783e-07 to 1.3369913e-06
Outputs:
- output: bfloat16 [256, 400, 432], P('img', 'band')
- input_grad: float32 [256, 400, 432], P('img', 'band')
- grad_norm: float32 [1], replicated
- grad_qkv: float32 [432, 1296], replicated
- grad_out: float32 [432, 432], replicated
- grad_fc1: float32 [432, 1728], replicated
- grad_fc2: float32 [1728, 432], replicated
- grad_gains: float32 [2, 432], replicated
- grad_biases: float32 [4, 432], replicated
- grad_fc1_bias: float32 [1728], replicated
- grad_head: float32 [4, 9], replicated
- new_qkv: float32 [432, 1296], replicated
- new_out: float32 [432, 432], replicated
- new_fc1: float32 [432, 1728], replicated
- new_fc2: float32 [1728, 432], replicated
- new_gains: float32 [2, 432], replicated
- new_biases: float32 [4, 432], replicated
- new_fc1_bias: float32 [1728], replicated
- new_head: float32 [4, 9], replicated
- new_rows_qkv: float32 [432], replicated
- new_cols_qkv: float32 [1296], replicated
- new_rows_out: float32 [432], replicated
- new_cols_out: float32 [432], replicated
- new_rows_fc1: float32 [432], replicated
- new_cols_fc1: float32 [1728], replicated
- new_rows_fc2: float32 [1728], replicated
- new_cols_fc2: float32 [432], replicated
- new_gain_moment: float32 [2, 432], replicated
- new_bias_moment: float32 [4, 432], replicated
- new_fc1_bias_moment: float32 [1728], replicated
- new_head_moment: float32 [4, 9], replicated
Inputs may be any that keep to these rules, and one draw needn't show every extreme that they name: `grid_sizes`: each value is 10, 14 or 18; every aligned block of 32 images holds a grid of 18 and a grid of 10. `head_params`: row 2 is negative.
All inputs are finite; a program needn't handle non-finite values.
Results may differ from a plain program's by a relative error of at most 0.02.
The roundings to bfloat16 on the way count: a program that leaves them out, or rounds other values in their place, can miss the bound.
Values may be sent and summed in bfloat16 or wider, within the bound.
A program may use at most 256 MiB of HBM per device.

v0:
```python
import functools
import math

import jax
import jax.numpy as jnp
import numpy as np
from jax import lax
from jax.experimental import pallas as pl
from jax.experimental.pallas import tpu as pltpu
from jax.sharding import PartitionSpec as P

GRID = 20
STEP = 10
SIDES = (18, 14, 10)

NORM_FLOOR = 1e-06
FLOOR_ONE = 1e-30
FLOOR_TWO = 0.001
STEP_RATE = 0.6
CLIP_RMS = 1.0
MASKED = -1e30

BF16 = jnp.bfloat16
F32 = jnp.float32
VMEM_LIMIT = 60 * 1024 * 1024
SUB = 16
SMALL_ROWS = 16
WAVES = 4
AXIS_ORDER = "cylhx"
LANE = 128


def round_up(value, unit):
    return (value + unit - 1) // unit * unit


def side_sizes(side):
    live = side * side
    return live, round_up(live, SUB), round_up(live, LANE)


def dot_nn(left, right):
    return lax.dot_general(left, right, (((1,), (0,)), ((), ())), preferred_element_type=F32)


def dot_nt(left, right):
    return lax.dot_general(left, right, (((1,), (1,)), ((), ())), preferred_element_type=F32)


def piece_rows(bands):
    return round_up(GRID // bands * max(SIDES), SUB)


def select_matrix(side, bands):
    live, rows, _ = side_sizes(side)
    tall, piece = GRID // bands, piece_rows(bands)
    made = np.zeros((rows, bands * piece), np.float32)
    for row in range(side):
        for col in range(side):
            at = row // tall * piece + (row % tall) * side + col
            made[row * side + col, at] = 1.0
    return made


def pack_matrix(bands):
    tall, piece = GRID // bands, piece_rows(bands)
    made = np.zeros((len(SIDES), piece, tall * GRID), np.float32)
    for index, side in enumerate(SIDES):
        for row in range(tall):
            for col in range(side):
                made[index, row * side + col, row * GRID + col] = 1.0
    return made


def fold_rows(values):
    rows, columns = values.shape
    return jnp.sum(values.reshape(rows // 8, 8, columns), axis=0)


def image_kernel(
    columns,
    heads,
    hidden_units,
    started,
    sizes_ref,
    gate_ref,
    xct_ref,
    tiles_in,
    small_in,
    sel_refs,
    selt_refs,
    place_hbm,
    weight_hbm,
    gains_ref,
    biases_ref,
    fc1b_ref,
    outig_ref,
    tiles_ref,
    small_ref,
    proj_s,
    projt_s,
    da_s,
    dat_s,
    cont_s,
    mix_s,
    attt_s,
    gt_s,
    act_s,
    gb_s,
    vec_s,
    fc1g_s,
    racc_s,
    gqkv_ref,
    gout_ref,
    g1_ref,
    g2t_ref,
    gsum_refs,
    gm_s,
    gc_s,
    place_refs,
    weight_refs,
    copy_sem,
):
    wqkv_ref, wback_ref, wout_ref, w1_ref, w2t_ref = weight_refs
    step = pl.program_id(0)
    steps = pl.num_programs(0)
    head_size = columns // heads
    width = wqkv_ref.shape[1] // 3
    window = 256
    score_scale = head_size ** (-0.5)
    chunk = 256
    chunks = w1_ref.shape[1] // chunk

    table = (gqkv_ref, gout_ref, g1_ref, g2t_ref)
    across = sum(ref.shape[1] // LANE for ref in table)
    row_tiles = columns // SUB

    sources = list(weight_hbm) + list(place_hbm)
    targets = list(weight_refs) + list(place_refs)
    loads = [
        pltpu.make_async_copy(source, target, copy_sem.at[1 + index])
        for index, (source, target) in enumerate(zip(sources, targets))
    ]
    load_qkv, load_back, load_out, load_w1, load_w2 = loads[:5]
    load_places = loads[5:]

    def once(*copies):
        @pl.when(step == 0)
        def _():
            for copy in copies:
                copy.wait()

    @pl.when(step == 0)
    def _():
        if started:
            load = pltpu.make_async_copy(tiles_in, tiles_ref, copy_sem.at[0])
            load.start()
        for copy in [load_qkv] + load_places + [load_out, load_w1, load_w2, load_back]:
            copy.start()
        if started:
            load.wait()

            def absorb(index, carry):
                at = pl.ds(pl.multiple_of(index * SUB, SUB), SUB)
                place = index * across
                for ref in table:
                    for col in range(ref.shape[1] // LANE):
                        ref[at, col * LANE : (col + 1) * LANE] = tiles_ref[place].astype(F32)
                        place = place + 1
                return carry

            lax.fori_loop(0, row_tiles, absorb, 0)
        else:
            for ref in table:
                ref[...] = jnp.zeros_like(ref)
        vec_s[...] = jnp.zeros_like(vec_s)
        fc1g_s[...] = jnp.zeros_like(fc1g_s)
        racc_s[...] = jnp.zeros_like(racc_s)
        for ref in gsum_refs:
            ref[...] = jnp.zeros_like(ref)

    def head_place(head):
        first_lane = head * head_size
        start = min(first_lane // LANE * LANE, width - window)
        lanes = lax.broadcasted_iota(jnp.int32, (1, window), 1) + start
        mask = (lanes >= first_lane) & (lanes < first_lane + head_size)
        return start, mask, first_lane

    def skewed(*stages):
        for index in range(heads + len(stages) - 1):
            for late, stage in enumerate(stages):
                if 0 <= index - late < heads:
                    stage(index - late)

    def image(side, sel_ref, selt_ref, place_ref, gsum_ref):
        live, rows, lanes = side_sizes(side)
        edge = live // 8 * 8
        tall = outig_ref.shape[3]

        def norm(values):
            averaged = jnp.mean(values, axis=-1, keepdims=True)
            centered = values - averaged
            variance = jnp.mean(centered * centered, axis=-1, keepdims=True)
            inverse = lax.rsqrt(variance + NORM_FLOOR)
            return centered * inverse, inverse

        def norm_back(grad, unit, inverse, gain):
            scaled = grad * gain
            first_mean = jnp.mean(scaled, axis=-1, keepdims=True)
            second_mean = jnp.mean(scaled * unit, axis=-1, keepdims=True)
            return inverse * (scaled - first_mean - unit * second_mean)

        x = dot_nn(sel_ref[...], xct_ref[:, 0, 0].reshape(-1, columns))
        unit_one, inverse_one = norm(x)
        first_b = (unit_one * gains_ref[0:1, :] + biases_ref[0:1, :]).astype(BF16)
        once(load_qkv)
        proj_s[:rows, :] = dot_nn(first_b, wqkv_ref[...]).astype(BF16)
        once(*load_places)
        if lanes > rows:
            proj_s[rows:lanes, :] = jnp.zeros((lanes - rows, 3 * width), BF16)
        for part in range(3):
            piece = proj_s[:lanes, part * width : (part + 1) * width]
            projt_s[part, :, :lanes] = piece.T

        def score_head(head):
            start, mask, row = head_place(head)
            query = jnp.where(mask, proj_s[:lanes, start : start + window], 0)
            key = proj_s[:rows, width + start : width + start + window]
            cont_s[head, :rows, :lanes] = dot_nt(key, query)

        def soft_head(head):
            score = cont_s[head, :rows, :lanes] * (score_scale * math.log2(math.e))
            tail = lax.broadcasted_iota(jnp.int32, (rows - edge, lanes), 0) < live - edge
            score = jnp.concatenate(
                [score[:edge], jnp.where(tail, score[edge:], MASKED)], axis=0
            )
            top = jnp.max(score, axis=0, keepdims=True)
            raised = jnp.exp2(score - top)
            total = jnp.sum(raised, axis=0, keepdims=True)
            content = raised * (gate_ref[head] / total)
            cont_s[head, :rows, :lanes] = content
            mix_s[head, :rows, :lanes] = (content + place_ref[head]).astype(BF16)

        def attend_head(head):
            row = head * head_size
            value_t = projt_s[2, row : row + head_size, :rows]
            mixed = mix_s[head, :rows, :lanes]
            attt_s[row : row + head_size, :lanes] = dot_nn(value_t, mixed).astype(BF16)

        skewed(score_head, soft_head, attend_head)

        once(load_out, load_w1, load_w2, load_back)
        attended = attt_s[:, :lanes].T[:rows]
        hidden = x + (dot_nn(attended, wout_ref[:columns, :]) + biases_ref[2:3, :])
        unit_two, inverse_two = norm(hidden)
        second_b = (unit_two * gains_ref[1:2, :] + biases_ref[1:2, :]).astype(BF16)
        ct_b = dot_nn(sel_ref[...], xct_ref[:, 1, 0].reshape(-1, columns)).astype(BF16)

        for index in range(chunks):
            at = slice(index * chunk, (index + 1) * chunk)
            before = dot_nn(second_b, w1_ref[:, at]) + fc1b_ref[:, at]
            grad_act = dot_nn(ct_b, w2t_ref[:, at])
            square = before * before
            inner = before * (
                math.sqrt(2.0 / math.pi) + (math.sqrt(2.0 / math.pi) * 0.044715) * square
            )
            half = 0.5 * jnp.tanh(inner) + 0.5
            activated = before * half
            slope = half + activated * (1.0 - half) * (
                2.0 * math.sqrt(2.0 / math.pi)
                + (6.0 * math.sqrt(2.0 / math.pi) * 0.044715) * square
            )
            act_s[:rows, at] = activated.astype(BF16)
            grad_b = (grad_act * slope).astype(BF16)
            gb_s[:rows, at] = grad_b
            fc1g_s[:, at] += fold_rows(grad_b.astype(F32))

        result = (
            hidden + dot_nt(act_s[:rows, :], w2t_ref[...]) + biases_ref[3:4, :]
        )
        outig_ref[:, 0, 0] = (
            dot_nn(selt_ref[...], result.astype(BF16)).astype(BF16).reshape(-1, tall, columns)
        )

        ct_t = ct_b.T
        second_t = second_b.T
        units = hidden_units
        for index in range(chunks):
            low, high = index * chunk, min((index + 1) * chunk, units)
            g1_ref[:, low:high] += dot_nn(second_t, gb_s[:rows, low:high])
            g2t_ref[:, low:high] += dot_nn(ct_t, act_s[:rows, low:high])

        ct_f = ct_b.astype(F32)
        grad_second = dot_nt(gb_s[:rows, :], w1_ref[...])
        grad_hidden = ct_f + norm_back(grad_second, unit_two, inverse_two, gains_ref[1:2, :])
        branch_b = grad_hidden.astype(BF16)
        vec_s[1] += fold_rows(grad_second * unit_two)
        vec_s[3] += fold_rows(grad_second)
        vec_s[4] += fold_rows(branch_b.astype(F32))
        vec_s[5] += fold_rows(ct_f)
        gout_ref[:, :columns] += dot_nn(attt_s[:, :rows], branch_b)
        da_s[:rows, :] = dot_nt(branch_b, wout_ref[...]).astype(BF16)
        if lanes > rows:
            da_s[rows:lanes, :] = jnp.zeros((lanes - rows, width), BF16)
        dat_s[:, :lanes] = da_s[:lanes, :].T

        def grad_head(head):
            start, mask, row = head_place(head)
            grad_att = jnp.where(mask, da_s[:lanes, start : start + window], 0)
            value = proj_s[:rows, 2 * width + start : 2 * width + start + window]
            gm_s[head % 2, :rows, :lanes] = dot_nt(value, grad_att)

        def soft_back_head(head):
            grad_mixed = gm_s[head % 2, :rows, :lanes]
            gsum_ref[head] += grad_mixed
            content = cont_s[head, :rows, :lanes]
            product = grad_mixed * content
            total = jnp.sum(product, axis=0, keepdims=True) / gate_ref[head]
            racc_s[head, :, :lanes] += total
            gc_s[head % 2, :rows, :lanes] = (product - content * total).astype(BF16)

        def back_head(head):
            row = head * head_size
            here = slice(row, row + head_size)
            mixed = mix_s[head, :rows, :lanes]
            grad_content = gc_s[head % 2, :rows, :lanes]
            gt_s[2 * columns + row : 2 * columns + row + head_size, :rows] = dot_nt(
                dat_s[here, :lanes], mixed
            ).astype(BF16)
            gt_s[columns + row : columns + row + head_size, :rows] = (
                dot_nt(projt_s[0, here, :lanes], grad_content) * score_scale
            ).astype(BF16)
            gt_s[here, :lanes] = (
                dot_nn(projt_s[1, here, :rows], grad_content) * score_scale
            ).astype(BF16)

        skewed(grad_head, soft_back_head, back_head)

        first_t = first_b.T
        grad_proj = gt_s[:, :lanes].T[:rows]
        gqkv_ref[:, : 3 * columns] += dot_nn(first_t, grad_proj)
        grad_first = dot_nt(grad_proj, wback_ref[...])
        vec_s[0] += fold_rows(grad_first * unit_one)
        vec_s[2] += fold_rows(grad_first)
        input_grad = grad_hidden + norm_back(grad_first, unit_one, inverse_one, gains_ref[0:1, :])
        outig_ref[:, 1, 0] = (
            dot_nn(selt_ref[...], input_grad.astype(BF16))
            .astype(BF16)
            .reshape(-1, tall, columns)
        )

    for index, side in enumerate(SIDES):

        @pl.when(sizes_ref[step] == side)
        def _(index=index, side=side):
            image(side, sel_refs[index], selt_refs[index], place_refs[index], gsum_refs[index])

    @pl.when(step == steps - 1)
    def _():
        def emit(index, carry):
            at = pl.ds(pl.multiple_of(index * SUB, SUB), SUB)
            place = index * across
            for ref in table:
                for col in range(ref.shape[1] // LANE):
                    tiles_ref[place] = ref[at, col * LANE : (col + 1) * LANE].astype(BF16)
                    place = place + 1
            return carry

        lax.fori_loop(0, row_tiles, emit, 0)
        for spare in range(row_tiles * across, tiles_ref.shape[0]):
            tiles_ref[spare] = jnp.zeros((SUB, LANE), BF16)

        small_ref[...] = jnp.zeros_like(small_ref)
        for row in range(6):
            small_ref[row : row + 1, :columns] = jnp.sum(vec_s[row], axis=0, keepdims=True)
        fc1_row = jnp.sum(fc1g_s[...], axis=0, keepdims=True)
        parts = hidden_units // columns
        for part in range(parts):
            small_ref[6 + part : 7 + part, :columns] = fc1_row[
                :, part * columns : (part + 1) * columns
            ]

        tile_rows = lax.broadcasted_iota(jnp.int32, (8, LANE), 0)
        tile_lanes = lax.broadcasted_iota(jnp.int32, (8, LANE), 1)
        grids = []
        for side in SIDES:
            rows, lanes = side_sizes(side)[1:]
            middle = 0.5 * (side - 1)
            key_ids = lax.broadcasted_iota(jnp.int32, (rows, LANE), 0).astype(F32)
            key_row = jnp.floor((key_ids + 0.5) * (1.0 / side))
            key_x, key_y = key_ids - side * key_row - middle, key_row - middle
            query_ids = lax.broadcasted_iota(jnp.int32, (1, lanes), 1).astype(F32)
            query_row = jnp.floor((query_ids + 0.5) * (1.0 / side))
            query_x, query_y = query_ids - side * query_row - middle, query_row - middle
            grids.append((key_x, key_y, key_x * key_x + key_y * key_y, query_x, query_y))

        def head_sums(head, carry):
            pieces = [jnp.zeros((1, LANE), F32) for _ in range(4)]
            gate_open = 1.0 - gate_ref[head]
            for index, side in enumerate(SIDES):
                lanes = side_sizes(side)[2]
                key_x, key_y, radius, query_x, query_y = grids[index]

                def total(values):
                    return jnp.sum(values, axis=0, keepdims=True)

                for strip in range(lanes // LANE):
                    at = slice(strip * LANE, (strip + 1) * LANE)
                    place = place_refs[index][head, :, at]
                    weighted = gsum_refs[index][head, :, at] * place
                    base = total(weighted)
                    scaled = base / gate_open
                    part_x = total(weighted * key_x) - total(place * key_x) * scaled
                    part_y = total(weighted * key_y) - total(place * key_y) * scaled
                    part_r = total(weighted * radius) - total(place * radius) * scaled
                    part_r -= 2.0 * (query_x[:, at] * part_x + query_y[:, at] * part_y)
                    for row, part in enumerate((part_x, part_y, part_r, gate_ref[head] * base)):
                        pieces[row] += part
            pieces = [jnp.sum(piece, axis=1, keepdims=True) for piece in pieces]
            pieces[3] -= gate_open * gate_ref[head] * jnp.sum(racc_s[head], axis=1, keepdims=True)
            for row in range(4):
                carry = carry + jnp.where(
                    (tile_rows == row) & (tile_lanes == head), pieces[row], 0.0
                )
            return carry

        head_tile = lax.fori_loop(0, heads, head_sums, jnp.zeros((8, LANE), F32))
        first_row = 6 + parts
        small_ref[first_row : first_row + 4, :LANE] = head_tile[:4]
        if started:
            small_ref[...] += small_in[...]


def run_images(xct, sizes, start, shared, previous, units, tile_count):
    bands, _, images, piece, columns = xct.shape
    places, gate_open, matrices, gains, biases, fc1b = shared
    heads = gate_open.shape[0]
    width = matrices[0].shape[1] // 3
    padded = matrices[3].shape[1]
    sels = [jnp.asarray(select_matrix(side, bands), BF16) for side in SIDES]
    selts = [jnp.asarray(select_matrix(side, bands).T, BF16) for side in SIDES]
    sizes_all = [side_sizes(side) for side in SIDES]
    most_rows = max(size[1] for size in sizes_all)
    most_lanes = max(size[2] for size in sizes_all)
    started = previous is not None

    def whole(array):
        rank = len(array.shape)
        return pl.BlockSpec(
            array.shape, lambda i, *_: (0,) * rank, pipeline_mode=pl.Buffered(1)
        )

    image_spec = pl.BlockSpec((bands, 2, 1, piece, columns), lambda i, *_: (0, 0, i, 0, 0))
    out_shapes = [
        jax.ShapeDtypeStruct(xct.shape, BF16),
        jax.ShapeDtypeStruct((tile_count, SUB, LANE), BF16),
        jax.ShapeDtypeStruct((SMALL_ROWS, width), F32),
    ]
    if not started:
        previous = (jnp.zeros((1, SUB, LANE), BF16), jnp.zeros((8, LANE), F32))
    scratch = [
        pltpu.VMEM((most_lanes, 3 * width), BF16),
        pltpu.VMEM((3, width, most_lanes), BF16),
        pltpu.VMEM((most_lanes, width), BF16),
        pltpu.VMEM((width, most_lanes), BF16),
        pltpu.VMEM((heads, most_rows, most_lanes), F32),
        pltpu.VMEM((heads, most_rows, most_lanes), BF16),
        pltpu.VMEM((columns, most_lanes), BF16),
        pltpu.VMEM((3 * columns, most_lanes), BF16),
        pltpu.VMEM((most_rows, padded), BF16),
        pltpu.VMEM((most_rows, padded), BF16),
        pltpu.VMEM((6, 8, columns), F32),
        pltpu.VMEM((8, padded), F32),
        pltpu.VMEM((heads, 1, most_lanes), F32),
        pltpu.VMEM((columns, round_up(3 * columns, LANE)), F32),
        pltpu.VMEM((columns, width), F32),
        pltpu.VMEM((columns, padded), F32),
        pltpu.VMEM((columns, padded), F32),
        [pltpu.VMEM((heads, size[1], size[2]), F32) for size in sizes_all],
        pltpu.VMEM((2, most_rows, most_lanes), F32),
        pltpu.VMEM((2, most_rows, most_lanes), BF16),
        [pltpu.VMEM(place.shape, F32) for place in places],
        [pltpu.VMEM(matrix.shape, BF16) for matrix in matrices],
        pltpu.SemaphoreType.DMA((1 + len(places) + len(matrices),)),
    ]
    smalls = [sels, selts, list(places), list(matrices), gains, biases, fc1b]
    body = functools.partial(image_kernel, columns, heads, units, started)
    hbm = lambda _: pl.BlockSpec(memory_space=pl.ANY)
    specs = [
        hbm(None),
        whole(previous[1]),
        jax.tree.map(whole, sels),
        jax.tree.map(whole, selts),
        [hbm(None) for _ in places],
        [hbm(None) for _ in matrices],
        whole(gains),
        whole(biases),
        whole(fc1b),
    ]
    return pl.pallas_call(
        body,
        grid_spec=pltpu.PrefetchScalarGridSpec(
            num_scalar_prefetch=2,
            grid=(images,),
            in_specs=[image_spec] + specs,
            out_specs=[image_spec] + [whole(shape) for shape in out_shapes[1:]],
            scratch_shapes=scratch,
        ),
        out_shape=out_shapes,
        compiler_params=pltpu.CompilerParams(vmem_limit_bytes=VMEM_LIMIT),
        cost_estimate=pl.CostEstimate(
            flops=images * 8_000_000_000, bytes_accessed=40_000_000, transcendentals=0
        ),
    )(lax.slice_in_dim(sizes, start, start + images), gate_open, xct, *previous, *smalls)


def lane_tiles(columns):
    return [
        (index, low, min(low + LANE, columns))
        for index, low in enumerate(range(0, columns, LANE))
    ]


def pack_kernel(chunks, order_ref, class_ref, x_ref, ct_ref, table_ref, *refs):
    outs, (wide_x, wide_ct) = refs[:-2], refs[-2:]
    band = pl.program_id(0)
    images = sum(chunks)
    rows, count, columns = x_ref.shape

    @pl.when(band == 0)
    def _():
        for source, wide in ((x_ref, wide_x), (ct_ref, wide_ct)):
            for index, low, high in lane_tiles(columns):
                wide[index, :, : high - low] = (
                    source[:, :, low:high].reshape(rows * count, high - low).astype(F32)
                )

    first = 0
    for out, size in zip(outs, chunks):

        def one(index, carry, out=out, first=first):
            place = band * images + first + index
            at = pl.ds(order_ref[place], rows, stride=count)
            select = table_ref[class_ref[place]]
            for which, wide in enumerate((wide_x, wide_ct)):
                for tile, low, high in lane_tiles(columns):
                    taken = dot_nn(select, wide[tile, at, :].astype(BF16)).astype(BF16)
                    out[0, which, index, :, low:high] = taken[:, : high - low]
            return carry

        lax.fori_loop(0, size, one, 0)
        first += size


def pack_images(x, ct, order, classes, bands, chunks):
    rows, count, columns = x.shape
    piece = piece_rows(bands)
    table = jnp.asarray(pack_matrix(bands), BF16)
    whole = lambda a: pl.BlockSpec(a.shape, lambda i, *_: (0, 0, 0), pipeline_mode=pl.Buffered(1))
    return pl.pallas_call(
        functools.partial(pack_kernel, chunks),
        grid_spec=pltpu.PrefetchScalarGridSpec(
            num_scalar_prefetch=2,
            grid=(bands,),
            in_specs=[whole(x), whole(ct), whole(table)],
            out_specs=[
                pl.BlockSpec((1, 2, size, piece, columns), lambda i, *_: (i, 0, 0, 0, 0))
                for size in chunks
            ],
            scratch_shapes=[pltpu.VMEM((round_up(columns, LANE) // LANE, rows * count, LANE), F32)] * 2,
        ),
        out_shape=[
            jax.ShapeDtypeStruct((bands, 2, size, piece, columns), BF16) for size in chunks
        ],
        compiler_params=pltpu.CompilerParams(vmem_limit_bytes=VMEM_LIMIT),
        cost_estimate=pl.CostEstimate(flops=10_000_000, bytes_accessed=14_000_000, transcendentals=0),
    )(order, classes, x, ct, table)


def unpack_kernel(chunks, order_ref, class_ref, table_ref, *refs):
    parts, (out_ref, ig_ref, wide_out, wide_ig) = refs[:-4], refs[-4:]
    band = pl.program_id(0)
    images = sum(chunks)
    rows, count, columns = out_ref.shape
    first = 0
    for part, size in zip(parts, chunks):

        def one(index, carry, part=part, first=first):
            place = band * images + first + index
            at = pl.ds(order_ref[place], rows, stride=count)
            spread = table_ref[class_ref[place]]
            for which, wide in enumerate((wide_out, wide_ig)):
                for tile, low, high in lane_tiles(columns):
                    made = dot_nn(spread, part[0, which, index, :, low:high])
                    if high - low < LANE:
                        fill = jnp.zeros((rows, LANE - (high - low)), F32)
                        made = jnp.concatenate([made, fill], axis=1)
                    wide[tile, at, :] = made
            return carry

        lax.fori_loop(0, size, one, 0)
        first += size

    @pl.when(band == pl.num_programs(0) - 1)
    def _():
        for target, wide in ((out_ref, wide_out), (ig_ref, wide_ig)):
            for tile, low, high in lane_tiles(columns):
                values = wide[tile, :, : high - low].astype(target.dtype)
                target[:, :, low:high] = values.reshape(rows, count, high - low)


def unpack_images(parts, order, classes, chunks, rows):
    bands, _, _, piece, columns = parts[0].shape
    count = bands * sum(chunks)
    table = jnp.asarray(pack_matrix(bands).transpose(0, 2, 1), BF16)
    whole = lambda a: pl.BlockSpec(a.shape, lambda i, *_: (0, 0, 0), pipeline_mode=pl.Buffered(1))
    outs = [
        jax.ShapeDtypeStruct((rows, count, columns), BF16),
        jax.ShapeDtypeStruct((rows, count, columns), F32),
    ]
    return pl.pallas_call(
        functools.partial(unpack_kernel, chunks),
        grid_spec=pltpu.PrefetchScalarGridSpec(
            num_scalar_prefetch=2,
            grid=(bands,),
            in_specs=[whole(table)]
            + [
                pl.BlockSpec((1, 2, size, piece, columns), lambda i, *_: (i, 0, 0, 0, 0))
                for size in chunks
            ],
            out_specs=[whole(shape) for shape in outs],
            scratch_shapes=[pltpu.VMEM((round_up(columns, LANE) // LANE, rows * count, LANE), F32)] * 2,
        ),
        out_shape=outs,
        compiler_params=pltpu.CompilerParams(vmem_limit_bytes=VMEM_LIMIT),
        cost_estimate=pl.CostEstimate(flops=10_000_000, bytes_accessed=16_000_000, transcendentals=0),
    )(order, classes, table, *parts)


def prep_kernel(head_ref, gate_ref, wqkv_in, wout_in, w1_in, w2t_in, *refs):
    wqkv, wback, wout, w1, w2t = refs[:5]
    places = refs[5:]
    columns = wout_in.shape[0]
    width = wout.shape[0]
    heads = head_ref.shape[1]
    wback[...] = wqkv_in[...].astype(BF16)
    for part in range(3):
        low = part * width
        wqkv[:, low : low + columns] = wqkv_in[:, part * columns : (part + 1) * columns].astype(BF16)
        wqkv[:, low + columns : low + width] = jnp.zeros((columns, width - columns), BF16)
    wout[:columns, :] = wout_in[...].astype(BF16)
    wout[columns:, :] = jnp.zeros((width - columns, columns), BF16)
    for out, source in ((w1, w1_in), (w2t, w2t_in)):
        units = source.shape[1]
        out[:, :units] = source[...].astype(BF16)
        out[:, units:] = jnp.zeros((columns, out.shape[1] - units), BF16)

    for side, place in zip(SIDES, places):
        live, rows, lanes = side_sizes(side)

        def spots(axis, rows=rows, lanes=lanes, side=side):
            ids = lax.broadcasted_iota(jnp.int32, (rows, lanes), axis)
            spot = ids.astype(F32)
            row = jnp.floor((spot + 0.5) * (1.0 / side))
            return ids, spot - side * row, row

        key_ids, key_x, key_y = spots(0)
        query_ids, query_x, query_y = spots(1)
        delta_x, delta_y = key_x - query_x, key_y - query_y
        distance = delta_x * delta_x + delta_y * delta_y
        dead_key = key_ids >= live
        inside = (key_ids < live) & (query_ids < live)

        def one(head, carry, place=place):
            scores = head_ref[0, head] * delta_x + head_ref[1, head] * delta_y
            scores = jnp.where(dead_key, MASKED, scores + head_ref[2, head] * distance)
            top = jnp.max(scores, axis=0, keepdims=True)
            raised = jnp.exp(scores - top)
            total = jnp.sum(raised, axis=0, keepdims=True)
            place[head] = jnp.where(inside, raised * (gate_ref[head] / total), 0.0)
            return carry

        lax.fori_loop(0, heads, one, 0)


def prepare(w_qkv, w_out, w_fc1, w_fc2t, head_params, gate_value):
    columns, heads = w_out.shape[0], head_params.shape[1]
    width = round_up(columns, LANE)
    padded = round_up(w_fc1.shape[1], 256)
    vmem = pl.BlockSpec(memory_space=pltpu.VMEM)
    smem = pl.BlockSpec(memory_space=pltpu.SMEM)
    shapes = [
        (columns, 3 * width),
        (columns, 3 * columns),
        (width, columns),
        (columns, padded),
        (columns, padded),
    ]
    outs = [jax.ShapeDtypeStruct(shape, BF16) for shape in shapes]
    outs += [jax.ShapeDtypeStruct((heads,) + side_sizes(side)[1:], F32) for side in SIDES]
    made = pl.pallas_call(
        prep_kernel,
        out_shape=outs,
        in_specs=[smem, smem] + [vmem] * 4,
        out_specs=[vmem] * len(outs),
        compiler_params=pltpu.CompilerParams(vmem_limit_bytes=VMEM_LIMIT),
        cost_estimate=pl.CostEstimate(
            flops=50_000_000, bytes_accessed=22_000_000, transcendentals=2_000_000
        ),
    )(head_params, gate_value, w_qkv, w_out, w_fc1, w_fc2t)
    return made[:5], made[5:]


def reduce_plan(tile_total, devices):
    each = -(-tile_total // devices)
    waves = []
    base = 0
    for wave in range(WAVES):
        share = each // WAVES + (1 if wave < each % WAVES else 0)
        if share:
            waves.append((base, share))
            base += devices * share
    return waves, each * devices


def reduce_kernel(
    waves,
    rank_z,
    own_ref,
    small_ref,
    full_out,
    small_out,
    own,
    full,
    recv0,
    recv1,
    small_own,
    small_recv,
    send_sem,
    recv_sem,
    small_send,
    small_got,
    copy_sem,
):
    img = lax.axis_index("img")
    band = lax.axis_index("band")
    z, y = img // 2, img % 2
    x, c = band // 2, band % 2
    low_z, high_z = z % 2, z // 2
    high_count = rank_z // 2
    mesh_ids = pl.DeviceIdType.MESH
    axes = {
        "c": (c, 2, lambda k: (img, x * 2 + 1 - c)),
        "y": (y, 2, lambda k: (z * 2 + 1 - y, band)),
        "x": (x, 2, lambda k: (img, (1 - x) * 2 + c)),
        "l": (low_z, 2, lambda k: ((high_z * 2 + 1 - low_z) * 2 + y, band)),
        "h": (
            high_z,
            high_count,
            lambda k: ((lax.rem(high_z + k, high_count) * 2 + low_z) * 2 + y, band),
        ),
    }
    order = [name for name in AXIS_ORDER if axes[name][1] > 1]
    partners = [axes[name][2](k) for name in order for k in range(1, axes[name][1])]
    devices = 1
    for name in order:
        devices *= axes[name][1]

    loads = []
    for w, (base, share) in enumerate(waves):
        at = pl.ds(base, devices * share)
        loads.append(pltpu.make_async_copy(own_ref.at[at], own.at[at], copy_sem.at[w]))
        loads[-1].start()
    small_own[...] = small_ref[...]

    barrier = pltpu.get_barrier_semaphore()
    for partner in partners:
        pl.semaphore_signal(barrier, inc=1, device_id=partner, device_id_type=mesh_ids)
    pl.semaphore_wait(barrier, len(partners))

    counters = [0] * len(waves)

    def send(wave, src, dst, target):
        slot = counters[wave]
        counters[wave] += 1
        copy = pltpu.make_async_remote_copy(
            src_ref=src,
            dst_ref=dst,
            send_sem=send_sem.at[wave, slot],
            recv_sem=recv_sem.at[wave, slot],
            device_id=target,
            device_id_type=mesh_ids,
        )
        copy.start()
        return copy

    def add_tiles(dst, dst_at, parts, count, out, out_at):
        block = 8

        def one(offset, size):
            total = dst[pl.ds(dst_at + offset, size)].astype(F32)
            for ref, at in parts:
                total += ref[pl.ds(at + offset, size)].astype(F32)
            out[pl.ds(out_at + offset, size)] = total.astype(BF16)

        if count >= block:

            def step(index, carry):
                one(index * block, block)
                return carry

            lax.fori_loop(0, count // block, step, 0)
        rest = count % block
        if rest:
            one(count - rest, rest)

    stores = []

    def wave_stages(w):
        base, share = waves[w]
        state = {"at": base, "size": devices * share, "copies": [], "parts": []}
        taken = [base // 2]

        def finish():
            for copy in state["copies"]:
                copy.wait()

        def scatter(name):
            def run():
                if state["parts"]:
                    finish()
                    add_tiles(own, state["at"], state["parts"], state["size"], own, state["at"])
                else:
                    loads[w].wait()
                mine, count, target = axes[name]
                size = state["size"] // count
                state["copies"], state["parts"] = [], []
                for k in range(1, count):
                    other = lax.rem(mine + k, count)
                    if name == order[0]:
                        buffer, at = recv0, base // 2
                    else:
                        buffer, at = recv1, taken[0]
                        taken[0] += size
                    state["copies"].append(
                        send(
                            w,
                            own.at[pl.ds(state["at"] + other * size, size)],
                            buffer.at[pl.ds(at, size)],
                            target(k),
                        )
                    )
                    state["parts"].append((buffer, at))
                state["at"] = state["at"] + mine * size
                state["size"] = size

            return run

        def gather(name, first):
            def run():
                finish()
                if first:
                    at = state["at"]
                    add_tiles(own, at, state["parts"], state["size"], full, at)
                mine, count, target = axes[name]
                piece = full.at[pl.ds(state["at"], state["size"])]
                state["copies"] = [send(w, piece, piece, target(k)) for k in range(1, count)]
                state["at"] = state["at"] - mine * state["size"]
                state["size"] = state["size"] * count

            return run

        def close():
            finish()
            at = pl.ds(base, devices * share)
            stores.append(
                pltpu.make_async_copy(full.at[at], full_out.at[at], copy_sem.at[len(waves) + w])
            )
            stores[-1].start()

        steps = [scatter(name) for name in order]
        steps += [gather(name, name == order[-1]) for name in reversed(order)]
        return steps + [close]

    small_slots = [0]
    small_state = {}

    def small_start(name):
        mine, count, target = axes[name]
        first = small_slots[0]
        small_slots[0] += count - 1
        small_state["copies"] = []
        for k in range(1, count):
            slot = first + k - 1
            copy = pltpu.make_async_remote_copy(
                src_ref=small_own,
                dst_ref=small_recv.at[slot],
                send_sem=small_send.at[slot],
                recv_sem=small_got.at[slot],
                device_id=target(k),
                device_id_type=mesh_ids,
            )
            copy.start()
            small_state["copies"].append(copy)
        small_state["first"] = first

    def small_end(name):
        mine, count, _ = axes[name]
        first = small_state["first"]
        for copy in small_state["copies"]:
            copy.wait()
        if count == 2:
            small_own[...] = small_own[...] + small_recv[first]
        else:
            last = small_recv.shape[0] - 1
            small_recv[last] = small_own[...]

            def add_line(index, total):
                k = lax.rem(mine - index + count, count)
                slot = jnp.where(k == 0, last, first + k - 1)
                return total + small_recv[slot]

            small_own[...] = lax.fori_loop(0, count, add_line, jnp.zeros_like(small_own))

    programs = [wave_stages(w) for w in range(len(waves))]
    depth = len(programs[0])
    for time in range(max(depth + len(waves) - 1, len(order) + 2)):
        for w in range(len(waves)):
            if 0 <= time - w < depth:
                programs[w][time - w]()
        if 1 <= time <= len(order) + 1:
            if time > 1:
                small_end(order[time - 2])
            if time <= len(order):
                small_start(order[time - 1])
    small_out[...] = small_own[...]
    for store in stores:
        store.wait()


def reduce_all(tiles, small, waves, img_count):
    total = tiles.shape[0]
    rank_z = img_count // 2
    copies = 2 * (4 + max(rank_z // 2 - 1, 0))
    hops = 4 + max(rank_z // 2 - 1, 0)
    return pl.pallas_call(
        functools.partial(reduce_kernel, waves, rank_z),
        out_shape=[
            jax.ShapeDtypeStruct(tiles.shape, BF16),
            jax.ShapeDtypeStruct(small.shape, F32),
        ],
        in_specs=[pl.BlockSpec(memory_space=pl.ANY), pl.BlockSpec(memory_space=pltpu.VMEM)],
        out_specs=[pl.BlockSpec(memory_space=pl.ANY), pl.BlockSpec(memory_space=pltpu.VMEM)],
        scratch_shapes=[
            pltpu.VMEM(tiles.shape, BF16),
            pltpu.VMEM(tiles.shape, BF16),
            pltpu.VMEM((total // 2, SUB, LANE), BF16),
            pltpu.VMEM((total // 2, SUB, LANE), BF16),
            pltpu.VMEM(small.shape, F32),
            pltpu.VMEM((hops + 1,) + small.shape, F32),
            pltpu.SemaphoreType.DMA((len(waves), copies)),
            pltpu.SemaphoreType.DMA((len(waves), copies)),
            pltpu.SemaphoreType.DMA((hops,)),
            pltpu.SemaphoreType.DMA((hops,)),
            pltpu.SemaphoreType.DMA((2 * len(waves),)),
        ],
        compiler_params=pltpu.CompilerParams(
            collective_id=1, has_side_effects=True, vmem_limit_bytes=VMEM_LIMIT
        ),
        cost_estimate=pl.CostEstimate(
            flops=10_000_000, bytes_accessed=200_000_000, transcendentals=0
        ),
    )(tiles, small)


def update_kernel(
    decay_rate,
    head_count,
    widths,
    tiles_ref,
    small_ref,
    weight_hbm,
    line_refs,
    vector_refs,
    moment_refs,
    norm_out,
    grad_hbm,
    new_hbm,
    vgrad_outs,
    vnew_outs,
    line_outs,
    moment_outs,
    weights,
    grads,
    news,
    row_s,
    col_s,
    copy_sem,
):
    columns = weights[0].shape[0]
    row_tiles = columns // SUB
    spans = [-(-wide // LANE) for wide in widths]
    total_span = tiles_stride(widths)
    starts = []
    at = 0
    for wide in widths:
        starts.append(at)
        at += tile_span(wide)
    loads = [
        pltpu.make_async_copy(weight_hbm[i], weights[i], copy_sem.at[i]) for i in range(4)
    ]
    for load in loads:
        load.start()

    def tile_rows(index, which):
        place = index * total_span + starts[which]
        pieces = [tiles_ref[place + col].astype(F32) for col in range(spans[which])]
        whole = jnp.concatenate(pieces, axis=1) if len(pieces) > 1 else pieces[0]
        return whole[:, : widths[which]]

    def all_sum(values):
        return jnp.sum(jnp.sum(values, axis=0, keepdims=True), axis=1, keepdims=True)

    def measure(index, carry):
        at = pl.ds(pl.multiple_of(index * SUB, SUB), SUB)
        made = []
        for which in range(4):
            grad = tile_rows(index, which)
            square = grad * grad
            row_s[which, at, :] = jnp.sum(square, axis=1, keepdims=True)
            made.append(carry[which] + fold_rows(square))
        return tuple(made)

    zeros = tuple(jnp.zeros((8, wide), F32) for wide in widths)
    folded = lax.fori_loop(0, row_tiles, measure, zeros)
    col_squares = [jnp.sum(fold, axis=0, keepdims=True) for fold in folded]
    total = jnp.zeros((1, 1), F32)
    for square in col_squares:
        total += jnp.sum(square, axis=1, keepdims=True)

    parts = vector_refs[2].shape[0]
    places = (
        (slice(0, 2), columns),
        (slice(2, 6), columns),
        (slice(6, 6 + parts), columns),
        (slice(6 + parts, 10 + parts), head_count),
    )
    vectors = [small_ref[rows, :wide] for rows, wide in places]
    for grad in vectors:
        total += all_sum(grad * grad)
    norm = jnp.sqrt(total)
    norm_out[...] = norm
    factor = 1.0 / jnp.maximum(norm, 1.0)

    for index in range(4):
        grad = vectors[index] * factor
        weight = vector_refs[index][...]
        moment = decay_rate * moment_refs[index][...] + (1.0 - decay_rate) * (
            grad * grad + FLOOR_ONE
        )
        update = grad * lax.rsqrt(moment)
        size = weight.shape[0] * weight.shape[1]
        mean_square = all_sum(update * update) / size
        update = update / jnp.maximum(1.0, jnp.sqrt(mean_square) / CLIP_RMS)
        scale = STEP_RATE * jnp.maximum(FLOOR_TWO, jnp.sqrt(all_sum(weight * weight) / size))
        vgrad_outs[index][...] = grad
        vnew_outs[index][...] = weight - scale * update
        moment_outs[index][...] = moment

    row_factors, col_factors = [], []
    for which in range(4):
        wide = widths[which]
        down_old, along_old = line_refs[which]
        down_out, along_out = line_outs[which]
        down = jnp.broadcast_to(down_old[...], (LANE, columns)).T
        down = decay_rate * down + (1.0 - decay_rate) * (
            row_s[which] * (factor * factor) / wide + FLOOR_ONE
        )
        along = decay_rate * along_old[...] + (1.0 - decay_rate) * (
            col_squares[which] * (factor * factor) / columns + FLOOR_ONE
        )
        down_out[...] = down.T[:1, :]
        along_out[...] = along
        down = down[:, :1]
        if which == 3:
            along = along / (jnp.sum(along, axis=1, keepdims=True) / wide)
        else:
            down = down / (jnp.sum(down, axis=0, keepdims=True) / columns)
        row_s[which] = lax.rsqrt(down) * factor
        col_s[which, :, :wide] = lax.rsqrt(along)

    for load in loads:
        load.wait()

    def scan(index, carry):
        at = pl.ds(pl.multiple_of(index * SUB, SUB), SUB)
        made = []
        for which in range(4):
            wide = widths[which]
            update = tile_rows(index, which) * col_s[which, :, :wide] * row_s[which, at, :]
            weight = weights[which][at, :]
            made.append(carry[2 * which] + fold_rows(update * update))
            made.append(carry[2 * which + 1] + fold_rows(weight * weight))
        return tuple(made)

    sums = lax.fori_loop(0, row_tiles, scan, tuple(z for z in zeros for _ in range(2)))
    stores = []
    for which in (2, 3, 0, 1):
        wide = widths[which]
        size = columns * wide
        scale = STEP_RATE * jnp.maximum(FLOOR_TWO, jnp.sqrt(all_sum(sums[2 * which + 1]) / size))
        scale = scale / jnp.maximum(1.0, jnp.sqrt(all_sum(sums[2 * which]) / size) / CLIP_RMS)
        col_factor = col_s[which, :, :wide] * scale

        def write(index, carry, which=which, col_factor=col_factor):
            at = pl.ds(pl.multiple_of(index * SUB, SUB), SUB)
            grad = tile_rows(index, which)
            grads[which][at, :] = grad * factor
            news[which][at, :] = weights[which][at, :] - grad * col_factor * row_s[which, at, :]
            return carry

        lax.fori_loop(0, row_tiles, write, 0)
        for source, target, slot in (
            (grads[which], grad_hbm[which], 4 + which),
            (news[which], new_hbm[which], 8 + which),
        ):
            stores.append(pltpu.make_async_copy(source, target, copy_sem.at[slot]))
            stores[-1].start()
    for store in stores:
        store.wait()


def tile_span(wide):
    return round_up(wide, 256 if wide > 1500 else LANE) // LANE


def tiles_stride(widths):
    return sum(tile_span(wide) for wide in widths)


def update_all(tiles, small, weights, rows, cols, vectors, moments, decay_rate):
    columns = weights[1].shape[0]
    head_count = vectors[3].shape[1]
    units = weights[2].shape[1]
    parts = units // columns
    flat = lambda v: v.reshape(1, -1)
    lines = [[flat(r), flat(c)] for r, c in zip(rows, cols)]
    lines[3] = lines[3][::-1]
    vectors = [v.reshape(parts, columns) if v.ndim == 1 else v for v in vectors]
    moments = [v.reshape(parts, columns) if v.ndim == 1 else v for v in moments]
    widths = [weight.shape[1] for weight in weights]
    like = lambda group: [jax.ShapeDtypeStruct(v.shape, F32) for v in group]
    outs = [
        jax.ShapeDtypeStruct((1, 1), F32),
        like(weights),
        like(weights),
        like(vectors),
        like(vectors),
        [like(pair) for pair in lines],
        like(vectors),
    ]
    vmem = pl.BlockSpec(memory_space=pltpu.VMEM)
    hbm = pl.BlockSpec(memory_space=pl.ANY)
    args = (tiles, small, list(weights), lines, vectors, moments)
    in_specs = list(jax.tree.map(lambda _: vmem, args))
    in_specs[2] = [hbm] * 4
    out_specs = jax.tree.map(lambda _: vmem, outs)
    out_specs[1] = [hbm] * 4
    out_specs[2] = [hbm] * 4
    full = lambda: [pltpu.VMEM(weight.shape, F32) for weight in weights]
    scratch = [
        full(),
        full(),
        full(),
        pltpu.VMEM((4, columns, 1), F32),
        pltpu.VMEM((4, 1, round_up(max(widths), LANE)), F32),
        pltpu.SemaphoreType.DMA((12,)),
    ]
    made = pl.pallas_call(
        functools.partial(update_kernel, decay_rate, head_count, widths),
        out_shape=outs,
        in_specs=in_specs,
        out_specs=out_specs,
        scratch_shapes=scratch,
        compiler_params=pltpu.CompilerParams(vmem_limit_bytes=VMEM_LIMIT),
    )(*args)
    norm, grads, news, vgrads, vnews, line_new, moment_new = made
    spread = lambda group: [v.reshape(-1) if i == 2 else v for i, v in enumerate(group)]
    line_new[3] = line_new[3][::-1]
    moved = [line.reshape(-1) for pair in line_new for line in pair]
    grads[3], news[3] = grads[3].T, news[3].T
    return (
        norm.reshape(1),
        *grads,
        *spread(vgrads),
        *news,
        *spread(vnews),
        *moved,
        *spread(moment_new),
    )


def deal_images(grid_sizes, devices):
    count = grid_sizes.shape[0]
    ids = jnp.arange(count, dtype=jnp.int32)
    ahead = (grid_sizes[None, :] > grid_sizes[:, None]) | (
        (grid_sizes[None, :] == grid_sizes[:, None]) & (ids[None, :] < ids[:, None])
    )
    rank = jnp.sum(ahead.astype(jnp.int32), axis=1)
    turn = rank // devices
    seat = rank % devices
    seat = jnp.where(turn % 2 == 0, seat, devices - 1 - seat)
    place = seat * (count // devices) + turn
    hit = place[None, :] == ids[:, None]
    order = jnp.sum(jnp.where(hit, ids[None, :], 0), axis=1)
    sizes = jnp.sum(jnp.where(hit, grid_sizes[None, :], 0), axis=1)
    return order, sizes


def per_device(
    inputs,
    cotangent,
    grid_sizes,
    w_qkv,
    w_out,
    w_fc1,
    w_fc2,
    norm_gains,
    biases,
    fc1_bias,
    head_params,
    rows_qkv,
    cols_qkv,
    rows_out,
    cols_out,
    rows_fc1,
    cols_fc1,
    rows_fc2,
    cols_fc2,
    gain_moment,
    bias_moment,
    fc1_bias_moment,
    head_moment,
):
    band_count = lax.axis_size("band")
    img_count = lax.axis_size("img")
    band_index = lax.axis_index("band")
    columns = inputs.shape[2]
    units = w_fc1.shape[1]
    per_band = inputs.shape[0] // band_count
    order, sizes_ordered = deal_images(grid_sizes, band_count)
    classes = sum(
        (jnp.where(sizes_ordered == side, index, 0) for index, side in enumerate(SIDES)),
        jnp.zeros_like(order),
    )
    sizes_used = lax.dynamic_slice_in_dim(sizes_ordered, band_index * per_band, per_band)
    early = max(1, per_band * 3 // 8)
    chunks = (early, per_band - early)
    packed = pack_images(
        jnp.swapaxes(inputs, 0, 1),
        jnp.swapaxes(cotangent, 0, 1),
        order,
        classes,
        band_count,
        chunks,
    )
    moved = [lax.all_to_all(part, "band", split_axis=0, concat_axis=0, tiled=True) for part in packed]
    waves, tile_count = reduce_plan(
        (columns // SUB) * tiles_stride((3 * columns, columns, units, units)),
        band_count * img_count,
    )
    w_fc2t = w_fc2.T
    gate_value = jax.nn.sigmoid(head_params[3])
    matrices, places = prepare(w_qkv, w_out, w_fc1, w_fc2t, head_params, gate_value)
    fc1b = jnp.pad(fc1_bias[None, :], ((0, 0), (0, matrices[3].shape[1] - units)))
    shared = (places, 1.0 - gate_value, matrices, norm_gains, biases, fc1b)
    previous = None
    start = 0
    results = []
    for part, size in zip(moved, chunks):
        result, *previous = run_images(part, sizes_used, start, shared, previous, units, tile_count)
        results.append(lax.all_to_all(result, "band", split_axis=0, concat_axis=0, tiled=True))
        start += size
    tiles, small = previous
    full, small = reduce_all(tiles, small, waves, img_count)
    updated = update_all(
        full,
        small,
        (w_qkv, w_out, w_fc1, w_fc2t),
        (rows_qkv, rows_out, rows_fc1, rows_fc2),
        (cols_qkv, cols_out, cols_fc1, cols_fc2),
        (norm_gains, biases, fc1_bias, head_params),
        (gain_moment, bias_moment, fc1_bias_moment, head_moment),
        1.0 - STEP ** (-0.8),
    )
    output, input_grad = unpack_images(results, order, classes, chunks, inputs.shape[1])
    return (jnp.swapaxes(output, 0, 1), jnp.swapaxes(input_grad, 0, 1), *updated)


def solution(mesh):
    split = P("img", "band", None)
    return jax.shard_map(
        per_device,
        mesh=mesh,
        in_specs=(split, split, P("img")) + (P(),) * 20,
        out_specs=(split, split) + (P(),) * 29,
        check_vma=False,
    )
```

profile of v0, /device:TPU:0, one launch (start us, length us, event | category | flops | bytes accessed | tf_op | source)
XLA Modules:
  0.0 394.8 jit_solution(10436074736430121796)
XLA Ops:
  0.7 0.9 convert_reduce_fusion
  1.6 1.3 select_reduce_fusion
  2.9 0.6 fusion.2.class_ref
  3.5 24.2 %shard_map.588 = (bf16[4,2,3,96,432]{4,3,2,1,0:T(8,128)(2,1)}, bf16[4,2,5,96,432]{4,3,2,1,0:T(8,128)(2,1)}) custom-call(s32[32]{0:T(128)} %get-tuple-element.130.order_ref, s32[32]{0:T(128)} %fusion.2.class_ref, bf16[100,32,432]{2,1,0:T(8,128)(2,1)} %bitcast.24, bf16[100,32,432]{2,1,0:T(8,128)(2,1)} %bitcast.25, bf16[3,96,100]{2,1,0:T(8,128)(2,1)} %constant.78.clone.table_ref), custom_call_target="tpu_custom_call" | custom-call | flops 10000000 | bytes 14000000 | tf_op jit(solution)/shard_map/pallas_call | solution.py:560
  27.7 33.6 %all_to_all.20.xct_ref = bf16[4,2,3,96,432]{4,3,2,1,0:T(8,128)(2,1)} all-to-all(bf16[4,2,3,96,432]{4,3,2,1,0:T(8,128)(2,1)} %get-tuple-element.80), channel_id=1, replica_groups=mesh['img'=8,'band'=4] {'band'}, dimensions={0} | all-to-all | bytes 3981312 | tf_op jit(solution)/shard_map/all_to_all | solution.py:1267
  61.3 0.0 copy-start.1
  61.3 4.9 %all-to-all-start.2 = ((bf16[4,2,5,96,432]{4,3,2,1,0:T(8,128)(2,1)}), bf16[4,2,5,96,432]{4,3,2,1,0:T(8,128)(2,1)}, u32[]{:S(2)}, u32[]{:S(2)}) async-start(bf16[4,2,5,96,432]{4,3,2,1,0:T(8,128)(2,1)} %get-tuple-element.90), calls=%async_computation.2 | async-start | bytes 7864320 | tf_op jit(solution)/shard_map/all_to_all | solution.py:1267
  66.2 0.1 dynamic_slice.3
  66.3 0.0 copy-start.6
  66.3 0.6 slice.11.sizes_ref
  66.9 0.0 copy-done.1
  66.9 0.6 pad.4.fc1b_ref
  67.5 1.2 broadcast_subtract_fusion
  68.7 13.9 %shard_map.589 = (bf16[432,1536]{1,0:T(8,128)(2,1)}, bf16[432,1296]{1,0:T(8,128)(2,1)}, bf16[512,432]{1,0:T(8,128)(2,1)}, bf16[432,1792]{1,0:T(8,128)(2,1)}, bf1...) custom-call(f32[4,9]{1,0:T(4,128)} %vector_refs_3_.1, ...), custom_call_target="tpu_custom_call" | custom-call | flops 50000000 | bytes 22000000 | tf_op jit(solution)/shard_map/pallas_call | solution.py:701
  82.6 0.0 copy-done.6
  82.6 0.6 broadcast_in_dim.42.tiles_in
  83.2 0.6 broadcast_in_dim.43.small_in
  83.8 72.1 %shard_map.590 = (bf16[4,2,3,96,432]{4,3,2,1,0:T(8,128)(2,1)}, bf16[1184,16,128]{2,1,0:T(8,128)(2,1)}, f32[16,512]{1,0:T(8,128)}) custom-call(s32[3]{0:T(128)} %bitcast.40, f32[9]{0:T(128)} %get-tuple-element.131.gate_ref, bf16[4,2,3,96,432]{4,3,2,1,0:T(8,128)(2,1)} %all_to_all.20.xct_ref, bf16[1,16,128]{2,1,0:T(8,128)(2,1)} %broadcast_in_dim.42.tiles_in, ...), custom_call_target="tpu_custom_call" | custom-call | flops 24000000000 | bytes 40000000 | tf_op jit(solution)/shard_map/pallas_call | solution.py:500
  155.8 0.0 all-to-all-done.2.xct_ref
  155.9 3.6 all-to-all-start.1
  159.5 57.2 %shard_map.591 = (bf16[4,2,5,96,432]{4,3,2,1,0:T(8,128)(2,1)}, bf16[1184,16,128]{2,1,0:T(8,128)(2,1)}, f32[16,512]{1,0:T(8,128)}) custom-call(s32[5]{0:T(128)} %slice.11.sizes_ref, f32[9]{0:T(128)} %get-tuple-element.131.gate_ref, bf16[4,2,5,96,432]{4,3,2,1,0:T(8,128)(2,1)} %all-to-all-done.2.xct_ref, bf16[1184,16,128]{2,1,0:T(8,128)(2,1)} %get-tuple-element.91.tiles_in, ...), custom_call_target="tpu_custom_call" | custom-call | flops 40000000000 | bytes 40000000 | tf_op jit(solution)/shard_map/pallas_call | solution.py:500
  216.7 0.0 all-to-all-done.1.refs_0_
  216.7 0.0 copy-start
  216.8 0.0 copy-start.2
  216.8 0.0 copy-start.4
  216.8 0.0 copy-start.5
  216.8 0.0 copy-start.3
  216.8 1.3 copy-done
  218.1 4.8 %all-to-all-start.3 = ((bf16[4,2,5,96,432]{4,3,2,1,0:T(8,128)(2,1)}), bf16[4,2,5,96,432]{4,3,2,1,0:T(8,128)(2,1)}, u32[]{:S(2)}, u32[]{:S(2)}) async-start(bf16[4,2,5,96,432]{4,3,2,1,0:T(8,128)(2,1)} %get-tuple-element.93), calls=%async_computation.3 | async-start | bytes 7864320 | tf_op jit(solution)/shard_map/all_to_all | solution.py:1282
  223.0 0.7 reshape.188.vector_refs_2_
  223.6 0.0 copy-done.2
  223.6 0.6 reshape.181.line_refs_0__1_
  224.2 0.0 copy-done.4
  224.2 0.6 reshape.185.line_refs_2__1_
  224.8 0.0 copy-done.5
  224.8 0.6 reshape.187.line_refs_3__1_
  225.4 0.0 copy-done.3
  225.4 0.7 reshape.189.moment_refs_2_
  226.1 111.5 %shard_map.593 = (bf16[1184,16,128]{2,1,0:T(8,128)(2,1)}, f32[16,512]{1,0:T(8,128)}) custom-call(bf16[1184,16,128]{2,1,0:T(8,128)(2,1)} %get-tuple-element.96.own_ref, f32[16,512]{1,0:T(8,128)} %get-tuple-element.97.small_ref), custom_call_target="tpu_custom_call" | custom-call | flops 10000000 | bytes 200000000 | tf_op jit(solution)/shard_map/pallas_call | solution.py:946
  337.6 21.9 %shard_map.594 = (f32[1,1]{1,0:T(1,128)}, f32[432,1296]{1,0:T(8,128)}, f32[432,432]{1,0:T(8,128)}, f32[432,1728]{1,0:T(8,128)}, f32[432,1728]{1,0:T(8,128)}, /*i...) custom-call(bf16[1184,16,128]{2,1,0:T(8,128)(2,1)} %get-tuple-elemen, ...), custom_call_target="tpu_custom_call" | custom-call | tf_op jit(solution)/shard_map/pallas_call | solution.py:1179
  359.5 1.4 reshape.191
  360.9 1.4 reshape.192
  362.3 1.3 reduce
  363.6 1.3 reduce.1
  364.9 1.3 reduce.2
  366.2 1.4 reshape.201
  367.6 0.0 all-to-all-done.3.refs_1_
  367.6 26.8 %shard_map.592 = (bf16[100,32,432]{2,1,0:T(8,128)(2,1)}, f32[100,32,432]{2,1,0:T(8,128)}) custom-call(s32[32]{0:T(128)} %get-tuple-element.130.order_ref, s32[32]{0:T(128)} %fusion.2.class_ref, bf16[3,100,96]{2,1,0:T(8,128)(2,1)} %constant.85.clone.table_ref, bf16[4,2,3,96,432]{4,3,2,1,0:T(8,128)(2,1)} %copy-done, ...), custom_call_target="tpu_custom_call" | custom-call | flops 10000000 | bytes 16000000 | tf_op jit(solution)/shard_map/pallas_call | solution.py:621
  (2 shorter events, 0.0 us)
Async XLA Ops:
  61.3 5.6 %copy-start.1 = (f32[1728]{0:T(1024)S(1)}, f32[1728]{0:T(1024)}, u32[]{:S(2)}) copy-start(f32[1728]{0:T(1024)} %param.46) | copy-start | bytes 20740
  61.3 94.6 %all-to-all-start.2 = ((bf16[4,2,5,96,432]{4,3,2,1,0:T(8,128)(2,1)}), bf16[4,2,5,96,432]{4,3,2,1,0:T(8,128)(2,1)}, u32[]{:S(2)}, u32[]{:S(2)}) async-start(bf16[4,2,5,96,432]{4,3,2,1,0:T(8,128)(2,1)} %get-tuple-element.90), calls=%async_computation.2 | async-start | bytes 7864320 | tf_op jit(solution)/shard_map/all_to_all | solution.py:1267
  66.3 16.3 %copy-start.6 = (s32[8]{0:T(128)}, s32[8]{0:T(128)S(1)}, u32[]{:S(2)}) copy-start(s32[8]{0:T(128)S(1)} %dynamic_slice.3) | copy-start | bytes 100
  155.9 60.9 %all-to-all-start.1 = ((bf16[4,2,3,96,432]{4,3,2,1,0:T(8,128)(2,1)}), bf16[4,2,3,96,432]{4,3,2,1,0:T(8,128)(2,1)S(1)}, u32[]{:S(2)}, u32[]{:S(2)}) async-start(bf16[4,2,3,96,432]{4,3,2,1,0:T(8,128)(2,1)} %get-tuple-element.89), calls=%async_computation.1 | async-start | bytes 4718592 | tf_op jit(solution)/shard_map/all_to_all | solution.py:1282
  216.7 1.4 copy-start
  216.8 6.9 %copy-start.2 = (f32[1296]{0:T(1024)S(1)}, f32[1296]{0:T(1024)}, u32[]{:S(2)}) copy-start(f32[1296]{0:T(1024)} %param.49) | copy-start | bytes 15556
  216.8 7.5 %copy-start.4 = (f32[1728]{0:T(1024)S(1)}, f32[1728]{0:T(1024)}, u32[]{:S(2)}) copy-start(f32[1728]{0:T(1024)} %param.53) | copy-start | bytes 20740
  216.8 8.1 %copy-start.5 = (f32[1728]{0:T(1024)S(1)}, f32[1728]{0:T(1024)}, u32[]{:S(2)}) copy-start(f32[1728]{0:T(1024)} %param.54) | copy-start | bytes 20740
  216.8 8.7 %copy-start.3 = (f32[1728]{0:T(1024)S(1)}, f32[1728]{0:T(1024)}, u32[]{:S(2)}) copy-start(f32[1728]{0:T(1024)} %param.58) | copy-start | bytes 20740
  218.1 149.4 %all-to-all-start.3 = ((bf16[4,2,5,96,432]{4,3,2,1,0:T(8,128)(2,1)}), bf16[4,2,5,96,432]{4,3,2,1,0:T(8,128)(2,1)}, u32[]{:S(2)}, u32[]{:S(2)}) async-start(bf16[4,2,5,96,432]{4,3,2,1,0:T(8,128)(2,1)} %get-tuple-element.93), calls=%async_computation.3 | async-start | bytes 7864320 | tf_op jit(solution)/shard_map/all_to_all | solution.py:1282
where the time goes:
time: 400 us; the launch traced here: 395 us
  Pallas kernels  328 us (82%)
  blocking collectives  33.6 us (8%)
  starting transfers between devices  13.3 us (3%)
  local copies, waits for them, and re-layouts  11.1 us (3%)
  other arithmetic  7.92 us (2%)
    pallas_call x2, Pallas kernels, run_images(): pl.pallas_call(body, grid_spec=pltpu.PrefetchScalarGridSpec(num_scalar_pr...  129 us
    pallas_call x1, Pallas kernels, reduce_all(): pl.pallas_call(functools.partial(reduce_kernel, waves, rank_z), out_shape...  111 us
    all_to_all x1, blocking collectives, per_device(): lax.all_to_all(part, 'band', split_axis=0, concat_axis=0, tiled=True)  33.6 us
    pallas_call x1, Pallas kernels, unpack_images(): pl.pallas_call(functools.partial(unpack_kernel, chunks), grid_spec=pltpu....  26.8 us
    pallas_call x1, Pallas kernels, pack_images(): pl.pallas_call(functools.partial(pack_kernel, chunks), grid_spec=pltpu.Pr...  24.2 us
    pallas_call x1, Pallas kernels, update_all(): pl.pallas_call(functools.partial(update_kernel, decay_rate, head_count, w...  21.9 us
    pallas_call x1, Pallas kernels, prepare(): pl.pallas_call(prep_kernel, out_shape=outs, in_specs=[smem, smem] + [vmem...  13.9 us
    all_to_all x2, starting transfers between devices, per_device(): lax.all_to_all(result, 'band', split_axis=0, concat_axis=0, tiled=True)  8.44 us
  transfers between devices with their start and end apart: 3, of which 0 were waited for; matrix products, arithmetic and copies ran while one was open for 4% of the time, Pallas kernels for 70%

commit v1 on v0

--- a/solution.py
+++ b/solution.py
@@ -25,8 +25,14 @@
 VMEM_LIMIT = 60 * 1024 * 1024
 SUB = 16
 SMALL_ROWS = 16
-WAVES = 4
-AXIS_ORDER = "cylhx"
+WAVES = (
+    ("cyxlh", 7, 0),
+    ("cxylh", 7, 0),
+    ("clhxy", 4, 0),
+    ("cyxlh", 7, 1),
+    ("cxylh", 7, 1),
+    ("clhxy", 5, 1),
+)
 LANE = 128
 
 
@@ -62,6 +68,12 @@
     return made
 
 
+def select_matrices(side, bands):
+    made = select_matrix(side, bands).reshape(-1, bands, piece_rows(bands))
+    ordered = [made[:, [own ^ step for step in range(bands)]] for own in range(bands)]
+    return np.stack(ordered).reshape(bands, made.shape[0], -1)
+
+
 def pack_matrix(bands):
     tall, piece = GRID // bands, piece_rows(bands)
     made = np.zeros((len(SIDES), piece, tall * GRID), np.float32)
@@ -81,20 +93,23 @@
     columns,
     heads,
     hidden_units,
+    image_count,
     started,
     sizes_ref,
+    band_ref,
     gate_ref,
-    xct_ref,
+    xct_refs,
     tiles_in,
     small_in,
     sel_refs,
     selt_refs,
     place_hbm,
+    moment_refs,
     weight_hbm,
     gains_ref,
     biases_ref,
     fc1b_ref,
-    outig_ref,
+    outig_refs,
     tiles_ref,
     small_ref,
     proj_s,
@@ -195,7 +210,16 @@
     def image(side, sel_ref, selt_ref, place_ref, gsum_ref):
         live, rows, lanes = side_sizes(side)
         edge = live // 8 * 8
-        tall = outig_ref.shape[3]
+        tall = outig_refs[0].shape[2]
+
+        def gathered(which):
+            pieces = jnp.concatenate([ref[which, 0] for ref in xct_refs], axis=0)
+            return dot_nn(sel_ref[0], pieces)
+
+        def spread(which, values):
+            values = dot_nn(selt_ref[0], values.astype(BF16)).astype(BF16)
+            for index, ref in enumerate(outig_refs):
+                ref[which, 0] = values[index * tall : (index + 1) * tall]
 
         def norm(values):
             averaged = jnp.mean(values, axis=-1, keepdims=True)
@@ -210,7 +234,7 @@
             second_mean = jnp.mean(scaled * unit, axis=-1, keepdims=True)
             return inverse * (scaled - first_mean - unit * second_mean)
 
-        x = dot_nn(sel_ref[...], xct_ref[:, 0, 0].reshape(-1, columns))
+        x = gathered(0)
         unit_one, inverse_one = norm(x)
         first_b = (unit_one * gains_ref[0:1, :] + biases_ref[0:1, :]).astype(BF16)
         once(load_qkv)
@@ -254,7 +278,7 @@
         hidden = x + (dot_nn(attended, wout_ref[:columns, :]) + biases_ref[2:3, :])
         unit_two, inverse_two = norm(hidden)
         second_b = (unit_two * gains_ref[1:2, :] + biases_ref[1:2, :]).astype(BF16)
-        ct_b = dot_nn(sel_ref[...], xct_ref[:, 1, 0].reshape(-1, columns)).astype(BF16)
+        ct_b = gathered(1).astype(BF16)
 
         for index in range(chunks):
             at = slice(index * chunk, (index + 1) * chunk)
@@ -278,9 +302,7 @@
         result = (
             hidden + dot_nt(act_s[:rows, :], w2t_ref[...]) + biases_ref[3:4, :]
         )
-        outig_ref[:, 0, 0] = (
-            dot_nn(selt_ref[...], result.astype(BF16)).astype(BF16).reshape(-1, tall, columns)
-        )
+        spread(0, result)
 
         ct_t = ct_b.T
         second_t = second_b.T
@@ -316,7 +338,7 @@
             content = cont_s[head, :rows, :lanes]
             product = grad_mixed * content
             total = jnp.sum(product, axis=0, keepdims=True) / gate_ref[head]
-            racc_s[head, :, :lanes] += total
+            racc_s[SIDES.index(side), head, :, :lanes] += total
             gc_s[head % 2, :rows, :lanes] = (product - content * total).astype(BF16)
 
         def back_head(head):
@@ -343,11 +365,7 @@
         vec_s[0] += fold_rows(grad_first * unit_one)
         vec_s[2] += fold_rows(grad_first)
         input_grad = grad_hidden + norm_back(grad_first, unit_one, inverse_one, gains_ref[0:1, :])
-        outig_ref[:, 1, 0] = (
-            dot_nn(selt_ref[...], input_grad.astype(BF16))
-            .astype(BF16)
-            .reshape(-1, tall, columns)
-        )
+        spread(1, input_grad)
 
     for index, side in enumerate(SIDES):
 
@@ -394,51 +412,67 @@
             query_x, query_y = query_ids - side * query_row - middle, query_row - middle
             grids.append((key_x, key_y, key_x * key_x + key_y * key_y, query_x, query_y))
 
-        def head_sums(head, carry):
+        def head_sums(index, head, carry):
             pieces = [jnp.zeros((1, LANE), F32) for _ in range(4)]
             gate_open = 1.0 - gate_ref[head]
-            for index, side in enumerate(SIDES):
-                lanes = side_sizes(side)[2]
-                key_x, key_y, radius, query_x, query_y = grids[index]
-
-                def total(values):
-                    return jnp.sum(values, axis=0, keepdims=True)
-
-                for strip in range(lanes // LANE):
-                    at = slice(strip * LANE, (strip + 1) * LANE)
-                    place = place_refs[index][head, :, at]
-                    weighted = gsum_refs[index][head, :, at] * place
-                    base = total(weighted)
-                    scaled = base / gate_open
-                    part_x = total(weighted * key_x) - total(place * key_x) * scaled
-                    part_y = total(weighted * key_y) - total(place * key_y) * scaled
-                    part_r = total(weighted * radius) - total(place * radius) * scaled
-                    part_r -= 2.0 * (query_x[:, at] * part_x + query_y[:, at] * part_y)
-                    for row, part in enumerate((part_x, part_y, part_r, gate_ref[head] * base)):
-                        pieces[row] += part
+            lanes = side_sizes(SIDES[index])[2]
+            key_x, key_y, radius, query_x, query_y = grids[index]
+
+            def total(values):
+                return jnp.sum(values, axis=0, keepdims=True)
+
+            for strip in range(lanes // LANE):
+                at = slice(strip * LANE, (strip + 1) * LANE)
+                weighted = gsum_refs[index][head, :, at] * place_refs[index][head, :, at]
+                base = total(weighted)
+                scaled = base / gate_open
+                mean_x, mean_y, mean_r = (
+                    moment_refs[index][head, row : row + 1, at] for row in range(3)
+                )
+                part_x = total(weighted * key_x) - mean_x * scaled
+                part_y = total(weighted * key_y) - mean_y * scaled
+                part_r = total(weighted * radius) - mean_r * scaled
+                part_r -= 2.0 * (query_x[:, at] * part_x + query_y[:, at] * part_y)
+                for row, part in enumerate((part_x, part_y, part_r, gate_ref[head] * base)):
+                    pieces[row] += part
             pieces = [jnp.sum(piece, axis=1, keepdims=True) for piece in pieces]
-            pieces[3] -= gate_open * gate_ref[head] * jnp.sum(racc_s[head], axis=1, keepdims=True)
+            rests = jnp.sum(racc_s[index, head], axis=1, keepdims=True)
+            pieces[3] -= gate_open * gate_ref[head] * rests
             for row in range(4):
                 carry = carry + jnp.where(
                     (tile_rows == row) & (tile_lanes == head), pieces[row], 0.0
                 )
             return carry
 
-        head_tile = lax.fori_loop(0, heads, head_sums, jnp.zeros((8, LANE), F32))
         first_row = 6 + parts
-        small_ref[first_row : first_row + 4, :LANE] = head_tile[:4]
+        for index, side in enumerate(SIDES):
+            present = sizes_ref[0] == side
+            for place in range(1, image_count):
+                present = present | (sizes_ref[place] == side)
+            @pl.when(present)
+            def _(index=index):
+                head_tile = lax.fori_loop(
+                    0,
+                    heads,
+                    functools.partial(head_sums, index),
+                    jnp.zeros((8, LANE), F32),
+                )
+                small_ref[first_row : first_row + 4, :LANE] += head_tile[:4]
+
         if started:
             small_ref[...] += small_in[...]
 
 
-def run_images(xct, sizes, start, shared, previous, units, tile_count):
-    bands, _, images, piece, columns = xct.shape
-    places, gate_open, matrices, gains, biases, fc1b = shared
+def run_images(xct, sizes, start, band, shared, previous, units, tile_count):
+    bands = len(xct)
+    _, images, piece, columns = xct[0].shape
+    places, moments, gate_open, matrices, gains, biases, fc1b = shared
     heads = gate_open.shape[0]
     width = matrices[0].shape[1] // 3
     padded = matrices[3].shape[1]
-    sels = [jnp.asarray(select_matrix(side, bands), BF16) for side in SIDES]
-    selts = [jnp.asarray(select_matrix(side, bands).T, BF16) for side in SIDES]
+    chosen = [select_matrices(side, bands) for side in SIDES]
+    sels = [jnp.asarray(made, BF16) for made in chosen]
+    selts = [jnp.asarray(made.transpose(0, 2, 1), BF16) for made in chosen]
     sizes_all = [side_sizes(side) for side in SIDES]
     most_rows = max(size[1] for size in sizes_all)
     most_lanes = max(size[2] for size in sizes_all)
@@ -450,9 +484,16 @@
             array.shape, lambda i, *_: (0,) * rank, pipeline_mode=pl.Buffered(1)
         )
 
-    image_spec = pl.BlockSpec((bands, 2, 1, piece, columns), lambda i, *_: (0, 0, i, 0, 0))
+    def own(array):
+        return pl.BlockSpec(
+            (1,) + array.shape[1:],
+            lambda i, sizes, band, *_: (band[0], 0, 0),
+            pipeline_mode=pl.Buffered(1),
+        )
+
+    image_specs = [pl.BlockSpec((2, 1, piece, columns), lambda i, *_: (0, i, 0, 0))] * bands
     out_shapes = [
-        jax.ShapeDtypeStruct(xct.shape, BF16),
+        [jax.ShapeDtypeStruct(part.shape, BF16) for part in xct],
         jax.ShapeDtypeStruct((tile_count, SUB, LANE), BF16),
         jax.ShapeDtypeStruct((SMALL_ROWS, width), F32),
     ]
@@ -471,7 +512,7 @@
         pltpu.VMEM((most_rows, padded), BF16),
         pltpu.VMEM((6, 8, columns), F32),
         pltpu.VMEM((8, padded), F32),
-        pltpu.VMEM((heads, 1, most_lanes), F32),
+        pltpu.VMEM((len(SIDES), heads, 1, most_lanes), F32),
         pltpu.VMEM((columns, round_up(3 * columns, LANE)), F32),
         pltpu.VMEM((columns, width), F32),
         pltpu.VMEM((columns, padded), F32),
@@ -483,15 +524,16 @@
         [pltpu.VMEM(matrix.shape, BF16) for matrix in matrices],
         pltpu.SemaphoreType.DMA((1 + len(places) + len(matrices),)),
     ]
-    smalls = [sels, selts, list(places), list(matrices), gains, biases, fc1b]
-    body = functools.partial(image_kernel, columns, heads, units, started)
+    smalls = [sels, selts, list(places), list(moments), list(matrices), gains, biases, fc1b]
+    body = functools.partial(image_kernel, columns, heads, units, images, started)
     hbm = lambda _: pl.BlockSpec(memory_space=pl.ANY)
     specs = [
         hbm(None),
         whole(previous[1]),
-        jax.tree.map(whole, sels),
-        jax.tree.map(whole, selts),
+        jax.tree.map(own, sels),
+        jax.tree.map(own, selts),
         [hbm(None) for _ in places],
+        jax.tree.map(whole, list(moments)),
         [hbm(None) for _ in matrices],
         whole(gains),
         whole(biases),
@@ -500,10 +542,10 @@
     return pl.pallas_call(
         body,
         grid_spec=pltpu.PrefetchScalarGridSpec(
-            num_scalar_prefetch=2,
+            num_scalar_prefetch=3,
             grid=(images,),
-            in_specs=[image_spec] + specs,
-            out_specs=[image_spec] + [whole(shape) for shape in out_shapes[1:]],
+            in_specs=[image_specs] + specs,
+            out_specs=[image_specs] + [whole(shape) for shape in out_shapes[1:]],
             scratch_shapes=scratch,
         ),
         out_shape=out_shapes,
@@ -511,7 +553,7 @@
         cost_estimate=pl.CostEstimate(
             flops=images * 8_000_000_000, bytes_accessed=40_000_000, transcendentals=0
         ),
-    )(lax.slice_in_dim(sizes, start, start + images), gate_open, xct, *previous, *smalls)
+    )(lax.slice_in_dim(sizes, start, start + images), band, gate_open, list(xct), *previous, *smalls)
 
 
 def lane_tiles(columns):
@@ -521,125 +563,122 @@
     ]
 
 
-def pack_kernel(chunks, order_ref, class_ref, x_ref, ct_ref, table_ref, *refs):
-    outs, (wide_x, wide_ct) = refs[:-2], refs[-2:]
-    band = pl.program_id(0)
-    images = sum(chunks)
+def pack_kernel(first, order_ref, class_ref, band_ref, x_ref, ct_ref, table_ref, *refs):
+    outs, wides = refs[:-2], refs[-2:]
     rows, count, columns = x_ref.shape
-
-    @pl.when(band == 0)
-    def _():
-        for source, wide in ((x_ref, wide_x), (ct_ref, wide_ct)):
+    images = count // len(outs)
+
+    for source, wide in zip((x_ref, ct_ref), wides):
+        for row in range(rows):
             for index, low, high in lane_tiles(columns):
-                wide[index, :, : high - low] = (
-                    source[:, :, low:high].reshape(rows * count, high - low).astype(F32)
-                )
-
-    first = 0
-    for out, size in zip(outs, chunks):
-
-        def one(index, carry, out=out, first=first):
-            place = band * images + first + index
-            at = pl.ds(order_ref[place], rows, stride=count)
+                at = slice(row * (count + 1), row * (count + 1) + count)
+                wide[index, at, : high - low] = source[row, :, low:high].astype(F32)
+
+    for step, out in enumerate(outs):
+
+        def one(index, carry, out=out, step=step):
+            place = (band_ref[0] ^ step) * images + first + index
+            at = pl.ds(order_ref[place], rows, stride=count + 1)
             select = table_ref[class_ref[place]]
-            for which, wide in enumerate((wide_x, wide_ct)):
+            for which, wide in enumerate(wides):
                 for tile, low, high in lane_tiles(columns):
                     taken = dot_nn(select, wide[tile, at, :].astype(BF16)).astype(BF16)
-                    out[0, which, index, :, low:high] = taken[:, : high - low]
+                    out[which, index, :, low:high] = taken[:, : high - low]
             return carry
 
-        lax.fori_loop(0, size, one, 0)
-        first += size
-
-
-def pack_images(x, ct, order, classes, bands, chunks):
+        lax.fori_loop(0, out.shape[1], one, 0)
+
+
+def pack_images(x, ct, order, classes, band, bands, first, size):
     rows, count, columns = x.shape
     piece = piece_rows(bands)
     table = jnp.asarray(pack_matrix(bands), BF16)
-    whole = lambda a: pl.BlockSpec(a.shape, lambda i, *_: (0, 0, 0), pipeline_mode=pl.Buffered(1))
+    vmem = pl.BlockSpec(memory_space=pltpu.VMEM)
     return pl.pallas_call(
-        functools.partial(pack_kernel, chunks),
+        functools.partial(pack_kernel, first),
         grid_spec=pltpu.PrefetchScalarGridSpec(
-            num_scalar_prefetch=2,
-            grid=(bands,),
-            in_specs=[whole(x), whole(ct), whole(table)],
-            out_specs=[
-                pl.BlockSpec((1, 2, size, piece, columns), lambda i, *_: (i, 0, 0, 0, 0))
-                for size in chunks
-            ],
-            scratch_shapes=[pltpu.VMEM((round_up(columns, LANE) // LANE, rows * count, LANE), F32)] * 2,
+            num_scalar_prefetch=3,
+            grid=(),
+            in_specs=[vmem] * 3,
+            out_specs=[vmem] * bands,
+            scratch_shapes=[
+                pltpu.VMEM(
+                    (round_up(columns, LANE) // LANE, round_up(rows * (count + 1), 8), LANE), F32
+                )
+            ]
+            * 2,
         ),
-        out_shape=[
-            jax.ShapeDtypeStruct((bands, 2, size, piece, columns), BF16) for size in chunks
-        ],
+        out_shape=[jax.ShapeDtypeStruct((2, size, piece, columns), BF16)] * bands,
         compiler_params=pltpu.CompilerParams(vmem_limit_bytes=VMEM_LIMIT),
-        cost_estimate=pl.CostEstimate(flops=10_000_000, bytes_accessed=14_000_000, transcendentals=0),
-    )(order, classes, x, ct, table)
-
-
-def unpack_kernel(chunks, order_ref, class_ref, table_ref, *refs):
-    parts, (out_ref, ig_ref, wide_out, wide_ig) = refs[:-4], refs[-4:]
-    band = pl.program_id(0)
+        cost_estimate=pl.CostEstimate(flops=10_000_000, bytes_accessed=10_000_000, transcendentals=0),
+    )(order, classes, band, x, ct, table)
+
+
+def unpack_kernel(chunks, bands, order_ref, class_ref, band_ref, table_ref, *refs):
+    parts, (out_ref, ig_ref), wides = refs[:-4], refs[-4:-2], refs[-2:]
     images = sum(chunks)
     rows, count, columns = out_ref.shape
     first = 0
-    for part, size in zip(parts, chunks):
-
-        def one(index, carry, part=part, first=first):
-            place = band * images + first + index
-            at = pl.ds(order_ref[place], rows, stride=count)
-            spread = table_ref[class_ref[place]]
-            for which, wide in enumerate((wide_out, wide_ig)):
-                for tile, low, high in lane_tiles(columns):
-                    made = dot_nn(spread, part[0, which, index, :, low:high])
-                    if high - low < LANE:
-                        fill = jnp.zeros((rows, LANE - (high - low)), F32)
-                        made = jnp.concatenate([made, fill], axis=1)
-                    wide[tile, at, :] = made
-            return carry
-
-        lax.fori_loop(0, size, one, 0)
+    for chunk, size in enumerate(chunks):
+        for step in range(bands):
+            part = parts[chunk * bands + step]
+
+            def one(index, carry, part=part, first=first, step=step):
+                place = (band_ref[0] ^ step) * images + first + index
+                at = pl.ds(order_ref[place], rows, stride=count + 1)
+                spread = table_ref[class_ref[place]]
+                for which, wide in enumerate(wides):
+                    for tile, low, high in lane_tiles(columns):
+                        made = dot_nn(spread, part[which, index, :, low:high])
+                        if high - low < LANE:
+                            fill = jnp.zeros((rows, LANE - (high - low)), F32)
+                            made = jnp.concatenate([made, fill], axis=1)
+                        wide[tile, at, :] = made
+                return carry
+
+            lax.fori_loop(0, size, one, 0)
         first += size
 
-    @pl.when(band == pl.num_programs(0) - 1)
-    def _():
-        for target, wide in ((out_ref, wide_out), (ig_ref, wide_ig)):
+    for target, wide in zip((out_ref, ig_ref), wides):
+        for row in range(rows):
             for tile, low, high in lane_tiles(columns):
-                values = wide[tile, :, : high - low].astype(target.dtype)
-                target[:, :, low:high] = values.reshape(rows, count, high - low)
-
-
-def unpack_images(parts, order, classes, chunks, rows):
-    bands, _, _, piece, columns = parts[0].shape
+                at = slice(row * (count + 1), row * (count + 1) + count)
+                target[row, :, low:high] = wide[tile, at, : high - low].astype(target.dtype)
+
+
+def unpack_images(parts, order, classes, band, chunks, rows):
+    bands = len(parts[0])
+    columns = parts[0][0].shape[-1]
     count = bands * sum(chunks)
     table = jnp.asarray(pack_matrix(bands).transpose(0, 2, 1), BF16)
-    whole = lambda a: pl.BlockSpec(a.shape, lambda i, *_: (0, 0, 0), pipeline_mode=pl.Buffered(1))
-    outs = [
-        jax.ShapeDtypeStruct((rows, count, columns), BF16),
-        jax.ShapeDtypeStruct((rows, count, columns), F32),
-    ]
+    vmem = pl.BlockSpec(memory_space=pltpu.VMEM)
+    flat = [piece for part in parts for piece in part]
     return pl.pallas_call(
-        functools.partial(unpack_kernel, chunks),
+        functools.partial(unpack_kernel, chunks, bands),
         grid_spec=pltpu.PrefetchScalarGridSpec(
-            num_scalar_prefetch=2,
-            grid=(bands,),
-            in_specs=[whole(table)]
-            + [
-                pl.BlockSpec((1, 2, size, piece, columns), lambda i, *_: (i, 0, 0, 0, 0))
-                for size in chunks
-            ],
-            out_specs=[whole(shape) for shape in outs],
-            scratch_shapes=[pltpu.VMEM((round_up(columns, LANE) // LANE, rows * count, LANE), F32)] * 2,
+            num_scalar_prefetch=3,
+            grid=(),
+            in_specs=[vmem] * (1 + len(flat)),
+            out_specs=[vmem] * 2,
+            scratch_shapes=[
+                pltpu.VMEM(
+                    (round_up(columns, LANE) // LANE, round_up(rows * (count + 1), 8), LANE), F32
+                )
+            ]
+            * 2,
         ),
-        out_shape=outs,
+        out_shape=[
+            jax.ShapeDtypeStruct((rows, count, columns), BF16),
+            jax.ShapeDtypeStruct((rows, count, columns), F32),
+        ],
         compiler_params=pltpu.CompilerParams(vmem_limit_bytes=VMEM_LIMIT),
         cost_estimate=pl.CostEstimate(flops=10_000_000, bytes_accessed=16_000_000, transcendentals=0),
-    )(order, classes, table, *parts)
+    )(order, classes, band, table, *flat)
 
 
 def prep_kernel(head_ref, gate_ref, wqkv_in, wout_in, w1_in, w2t_in, *refs):
     wqkv, wback, wout, w1, w2t = refs[:5]
-    places = refs[5:]
+    places, moments = refs[5:8], refs[8:11]
     columns = wout_in.shape[0]
     width = wout.shape[0]
     heads = head_ref.shape[1]
@@ -655,7 +694,7 @@
         out[:, :units] = source[...].astype(BF16)
         out[:, units:] = jnp.zeros((columns, out.shape[1] - units), BF16)
 
-    for side, place in zip(SIDES, places):
+    for side, place, moment in zip(SIDES, places, moments):
         live, rows, lanes = side_sizes(side)
 
         def spots(axis, rows=rows, lanes=lanes, side=side):
@@ -670,14 +709,19 @@
         distance = delta_x * delta_x + delta_y * delta_y
         dead_key = key_ids >= live
         inside = (key_ids < live) & (query_ids < live)
-
-        def one(head, carry, place=place):
+        middle = 0.5 * (side - 1)
+        from_x, from_y = key_x - middle, key_y - middle
+
+        def one(head, carry, place=place, moment=moment, from_x=from_x, from_y=from_y):
             scores = head_ref[0, head] * delta_x + head_ref[1, head] * delta_y
             scores = jnp.where(dead_key, MASKED, scores + head_ref[2, head] * distance)
             top = jnp.max(scores, axis=0, keepdims=True)
             raised = jnp.exp(scores - top)
             total = jnp.sum(raised, axis=0, keepdims=True)
-            place[head] = jnp.where(inside, raised * (gate_ref[head] / total), 0.0)
+            made = jnp.where(inside, raised * (gate_ref[head] / total), 0.0)
+            place[head] = made
+            for row, factor in enumerate((from_x, from_y, from_x * from_x + from_y * from_y)):
+                moment[head, row : row + 1, :] = jnp.sum(made * factor, axis=0, keepdims=True)
             return carry
 
         lax.fori_loop(0, heads, one, 0)
@@ -698,6 +742,7 @@
     ]
     outs = [jax.ShapeDtypeStruct(shape, BF16) for shape in shapes]
     outs += [jax.ShapeDtypeStruct((heads,) + side_sizes(side)[1:], F32) for side in SIDES]
+    outs += [jax.ShapeDtypeStruct((heads, 8, side_sizes(side)[2]), F32) for side in SIDES]
     made = pl.pallas_call(
         prep_kernel,
         out_shape=outs,
@@ -708,18 +753,21 @@
             flops=50_000_000, bytes_accessed=22_000_000, transcendentals=2_000_000
         ),
     )(head_params, gate_value, w_qkv, w_out, w_fc1, w_fc2t)
-    return made[:5], made[5:]
+    return made[:5], made[5:8], made[8:]
 
 
 def reduce_plan(tile_total, devices):
     each = -(-tile_total // devices)
+    weight = sum(wave[1] for wave in WAVES)
     waves = []
-    base = 0
-    for wave in range(WAVES):
-        share = each // WAVES + (1 if wave < each % WAVES else 0)
+    base = before = taken = 0
+    for order, part, start in WAVES:
+        before += part
+        share = -(-each * before // weight) - taken
         if share:
-            waves.append((base, share))
+            waves.append((base, share, order, start))
             base += devices * share
+            taken += share
     return waves, each * devices
 
 
@@ -760,14 +808,14 @@
             lambda k: ((lax.rem(high_z + k, high_count) * 2 + low_z) * 2 + y, band),
         ),
     }
-    order = [name for name in AXIS_ORDER if axes[name][1] > 1]
+    order = [name for name in "cyxlh" if axes[name][1] > 1]
     partners = [axes[name][2](k) for name in order for k in range(1, axes[name][1])]
     devices = 1
     for name in order:
         devices *= axes[name][1]
 
     loads = []
-    for w, (base, share) in enumerate(waves):
+    for w, (base, share, _, _) in enumerate(waves):
         at = pl.ds(base, devices * share)
         loads.append(pltpu.make_async_copy(own_ref.at[at], own.at[at], copy_sem.at[w]))
         loads[-1].start()
@@ -817,7 +865,8 @@
     stores = []
 
     def wave_stages(w):
-        base, share = waves[w]
+        base, share, axis_order, _ = waves[w]
+        order = [name for name in axis_order if axes[name][1] > 1]
         state = {"at": base, "size": devices * share, "copies": [], "parts": []}
         taken = [base // 2]
 
@@ -924,10 +973,13 @@
 
     programs = [wave_stages(w) for w in range(len(waves))]
     depth = len(programs[0])
-    for time in range(max(depth + len(waves) - 1, len(order) + 2)):
-        for w in range(len(waves)):
-            if 0 <= time - w < depth:
-                programs[w][time - w]()
+    for program in programs:
+        program[0]()
+    last = max(wave[3] for wave in waves) + depth
+    for time in range(1, max(last, len(order) + 2)):
+        for w, wave in enumerate(waves):
+            if 1 <= time - wave[3] < depth:
+                programs[w][time - wave[3]]()
         if 1 <= time <= len(order) + 1:
             if time > 1:
                 small_end(order[time - 2])
@@ -1254,35 +1306,50 @@
         jnp.zeros_like(order),
     )
     sizes_used = lax.dynamic_slice_in_dim(sizes_ordered, band_index * per_band, per_band)
-    early = max(1, per_band * 3 // 8)
+    early = max(1, per_band // 2)
     chunks = (early, per_band - early)
-    packed = pack_images(
-        jnp.swapaxes(inputs, 0, 1),
-        jnp.swapaxes(cotangent, 0, 1),
-        order,
-        classes,
-        band_count,
-        chunks,
+    band = band_index.astype(jnp.int32).reshape(1)
+    x_stored, ct_stored = jnp.swapaxes(inputs, 0, 1), jnp.swapaxes(cotangent, 0, 1)
+    pack = lambda first, size: pack_images(
+        x_stored, ct_stored, order, classes, band, band_count, first, size
     )
-    moved = [lax.all_to_all(part, "band", split_axis=0, concat_axis=0, tiled=True) for part in packed]
+
+    def exchange(parts):
+        swaps = [[(i, i ^ step) for i in range(band_count)] for step in range(band_count)]
+        return [parts[0]] + [
+            lax.ppermute(parts[step], "band", swaps[step]) for step in range(1, band_count)
+        ]
+
     waves, tile_count = reduce_plan(
         (columns // SUB) * tiles_stride((3 * columns, columns, units, units)),
         band_count * img_count,
     )
     w_fc2t = w_fc2.T
     gate_value = jax.nn.sigmoid(head_params[3])
-    matrices, places = prepare(w_qkv, w_out, w_fc1, w_fc2t, head_params, gate_value)
+    matrices, places, spots = prepare(w_qkv, w_out, w_fc1, w_fc2t, head_params, gate_value)
+    first_part = pack(0, early)
+    first_moved = exchange(first_part)
+    later_part = pack(early, per_band - early)
+    later_part, matrices, first_moved = lax.optimization_barrier(
+        (later_part, matrices, first_moved)
+    )
+    moved = [first_moved, exchange(later_part)]
     fc1b = jnp.pad(fc1_bias[None, :], ((0, 0), (0, matrices[3].shape[1] - units)))
-    shared = (places, 1.0 - gate_value, matrices, norm_gains, biases, fc1b)
+    shared = (places, spots, 1.0 - gate_value, matrices, norm_gains, biases, fc1b)
     previous = None
     start = 0
     results = []
     for part, size in zip(moved, chunks):
-        result, *previous = run_images(part, sizes_used, start, shared, previous, units, tile_count)
-        results.append(lax.all_to_all(result, "band", split_axis=0, concat_axis=0, tiled=True))
+        result, *previous = run_images(
+            part, sizes_used, start, band, shared, previous, units, tile_count
+        )
+        results.append(result)
         start += size
     tiles, small = previous
+    results[0], tiles = lax.optimization_barrier((exchange(results[0]), tiles))
     full, small = reduce_all(tiles, small, waves, img_count)
+    results[1], full = lax.optimization_barrier((results[1], full))
+    results[1] = exchange(results[1])
     updated = update_all(
         full,
         small,
@@ -1293,7 +1360,9 @@
         (gain_moment, bias_moment, fc1_bias_moment, head_moment),
         1.0 - STEP ** (-0.8),
     )
-    output, input_grad = unpack_images(results, order, classes, chunks, inputs.shape[1])
+    output, input_grad = unpack_images(
+        results, order, classes, band, chunks, inputs.shape[1]
+    )
     return (jnp.swapaxes(output, 0, 1), jnp.swapaxes(input_grad, 0, 1), *updated)
 
 

time: 400 us -> 315 us (0.79)
  Pallas kernels: 328 us -> 274 us
  blocking collectives: 33.6 us -> 0 us
  waiting for transfers between devices: 0.01 us -> 8.73 us
  starting transfers between devices: 13.3 us -> 8.8 us
    pallas_call x1, Pallas kernels: 111 us -> 71.2 us  [reduce_all(): pl.pallas_call(functools.partial(reduce_kernel, waves, rank_z), out_shape...]
    all_to_all x1 -> x0, blocking collectives: 33.6 us -> none  [per_device(): lax.all_to_all(part, 'band', split_axis=0, concat_axis=0, tiled=True)]
    pallas_call x2 -> x3, Pallas kernels: 51 us -> 35 us  [the longest x2 18.7 us: pack_images(): pl.pallas_call(functools.partial(pack_kernel, first), grid_spec=pltpu.Pre...]
    all_to_all x3 -> x0, starting transfers between devices: 13.3 us -> none  [the longest x2 8.44 us: per_device(): lax.all_to_all(result, 'band', split_axis=0, concat_axis=0, tiled=True)]
    ppermute x0 -> x12, starting transfers between devices: none -> 8.8 us  [exchange(): lax.ppermute(parts[step], 'band', swaps[step])]
    ppermute x0 -> x12, waiting for transfers between devices: none -> 8.73 us  [exchange(): lax.ppermute(parts[step], 'band', swaps[step])]
  transfers between devices with their start and end apart: 3 -> 12, of which waited for: 0 -> 2; matrix products, arithmetic and copies ran while one was open for 4% -> 5% of each run, Pallas kernels for 70% -> 57%
where the time goes in v1:
time: 315 us; the launch traced here: 311 us
  Pallas kernels  274 us (87%)
  local copies, waits for them, and re-layouts  9.79 us (3%)
  starting transfers between devices  8.8 us (3%)
  waiting for transfers between devices  8.73 us (3%)
  other arithmetic  7.92 us (3%)
    pallas_call x2, Pallas kernels, run_images(): pl.pallas_call(body, grid_spec=pltpu.PrefetchScalarGridSpec(num_scalar_pr...  131 us
    pallas_call x1, Pallas kernels, reduce_all(): pl.pallas_call(functools.partial(reduce_kernel, waves, rank_z), out_shape...  71.2 us
    pallas_call x1, Pallas kernels, update_all(): pl.pallas_call(functools.partial(update_kernel, decay_rate, head_count, w...  21.8 us
    pallas_call x2, Pallas kernels, pack_images(): pl.pallas_call(functools.partial(pack_kernel, first), grid_spec=pltpu.Pre...  18.7 us
    pallas_call x1, Pallas kernels, unpack_images(): pl.pallas_call(functools.partial(unpack_kernel, chunks, bands), grid_spec...  16.2 us
    pallas_call x1, Pallas kernels, prepare(): pl.pallas_call(prep_kernel, out_shape=outs, in_specs=[smem, smem] + [vmem...  15.8 us
    ppermute x12, starting transfers between devices, exchange(): lax.ppermute(parts[step], 'band', swaps[step])  8.8 us
    ppermute x12, waiting for transfers between devices, exchange(): lax.ppermute(parts[step], 'band', swaps[step])  8.73 us
  transfers between devices with their start and end apart: 12, of which 2 were waited for; matrix products, arithmetic and copies ran while one was open for 5% of the time, Pallas kernels for 57%

profile of v1, /device:TPU:0, one launch (start us, length us, event | category | flops | bytes accessed | tf_op | source)
XLA Modules:
  0.0 311.0 jit_solution(655626696566008554)
XLA Ops:
  0.7 0.9 convert_reduce_fusion
  1.6 1.3 select_reduce_fusion
  2.9 0.5 fusion.2.class_ref
  3.5 9.4 %shard_map.599 = (bf16[2,4,96,432]{3,2,1,0:T(8,128)(2,1)}, bf16[2,4,96,432]{3,2,1,0:T(8,128)(2,1)}, bf16[2,4,96,432]{3,2,1,0:T(8,128)(2,1)}, bf16[2,4,96,432]{3,2,1,0:T(8,128)(2,1)}) custom-call(s32[32]{0:T(128)} %get-tuple-element.206.order_ref, s32[32]{0:T(128)} %fusion.2.class_ref, s32[1]{0:T(128)} %bitcast.band_ref, bf16[100,32,432]{2,1,0:T(8,128)(2,1)} %bitcast.22, ...), custom_call_target="tpu_custom_call" | custom-call | flops 10000000 | bytes 10000000 | tf_op jit(solution)/shard_map/pallas_call | solution.py:597
  12.9 0.5 collective-permute-start
  13.3 2.5 collective-permute-start.1
  15.8 0.1 collective-permute-start.2
  16.0 0.1 dynamic_slice.3
  16.0 0.0 copy-done.4
  16.1 0.6 pad.4.fc1b_ref
  16.7 9.3 %shard_map.597 = (bf16[2,4,96,432]{3,2,1,0:T(8,128)(2,1)}, bf16[2,4,96,432]{3,2,1,0:T(8,128)(2,1)}, bf16[2,4,96,432]{3,2,1,0:T(8,128)(2,1)}, bf16[2,4,96,432]{3,2,1,0:T(8,128)(2,1)}) custom-call(s32[32]{0:T(128)} %get-tuple-element.206.order_ref, s32[32]{0:T(128)} %fusion.2.class_ref, s32[1]{0:T(128)} %bitcast.band_ref, bf16[100,32,432]{2,1,0:T(8,128)(2,1)} %bitcast.23, ...), custom_call_target="tpu_custom_call" | custom-call | flops 10000000 | bytes 10000000 | tf_op jit(solution)/shard_map/pallas_call | solution.py:597
  26.0 1.2 broadcast_subtract_fusion
  27.2 15.8 %shard_map.598 = (bf16[432,1536]{1,0:T(8,128)(2,1)}, bf16[432,1296]{1,0:T(8,128)(2,1)}, bf16[512,432]{1,0:T(8,128)(2,1)}, bf16[432,1792]{1,0:T(8,128)(2,1)}, bf1...) custom-call(f32[4,9]{1,0:T(4,128)} %vector_refs_3_.1, ...), custom_call_target="tpu_custom_call" | custom-call | flops 50000000 | bytes 22000000 | tf_op jit(solution)/shard_map/pallas_call | solution.py:746
  43.0 0.6 fusion.4
  43.6 0.0 collective-permute-done.xct_refs_1_
  43.6 0.0 collective-permute-done.1.xct_refs_2_
  43.6 0.0 copy-start.11
  43.6 7.3 %collective-permute-done.2.xct_refs_3_ = bf16[2,4,96,432]{3,2,1,0:T(8,128)(2,1)S(1)} collective-permute-done((bf16[2,4,96,432]{3,2,1,0:T(8,128)(2,1)}, bf16[2,4,96,432]{3,2,1,0:T(8,128)(2,1)S(1)}, u32[]{:S(2)}, u32[]{:S(2)}) %collective-permute-start.2) | collective-permute-done | bytes 663584 | tf_op jit(solution)/shard_map/ppermute | solution.py:1320
  50.9 0.1 collective-permute-start.6
  51.0 1.6 collective-permute-start.7
  52.7 0.0 copy-done.10
  52.7 0.1 collective-permute-start.8
  52.8 0.6 broadcast_in_dim.42.tiles_in
  53.4 0.6 broadcast_in_dim.43.small_in
  54.0 0.0 copy-done.9
  54.0 0.0 copy-done.11
  54.0 0.0 copy-done.12
  54.0 86.2 %shard_map.600 = (bf16[2,4,96,432]{3,2,1,0:T(8,128)(2,1)}, bf16[2,4,96,432]{3,2,1,0:T(8,128)(2,1)}, bf16[2,4,96,432]{3,2,1,0:T(8,128)(2,1)}, bf16[2,4,96,432]{3,...) custom-call(s32[4]{0:T(128)} %get-tuple-element.210.sizes_ref, s32[1]{0:T(128)} %bitcast.band_ref, ...), custom_call_target="tpu_custom_call" | custom-call | flops 32000000000 | bytes 40000000 | tf_op jit(solution)/shard_map/pallas_call | solution.py:542
  140.2 0.5 collective-permute-start.3
  140.7 1.2 collective-permute-start.4
  141.9 0.0 collective-permute-done.6.xct_refs_1_
  141.9 0.3 collective-permute-start.5
  142.1 0.0 collective-permute-done.7.xct_refs_2_
  142.1 0.0 collective-permute-done.8.xct_refs_3_
  142.1 44.5 %shard_map.601 = (bf16[2,4,96,432]{3,2,1,0:T(8,128)(2,1)}, bf16[2,4,96,432]{3,2,1,0:T(8,128)(2,1)}, bf16[2,4,96,432]{3,2,1,0:T(8,128)(2,1)}, bf16[2,4,96,432]{3,...) custom-call(s32[4]{0:T(128)} %get-tuple-element.209.sizes_ref, s32[1]{0:T(128)} %bitcast.band_ref, ...), custom_call_target="tpu_custom_call" | custom-call | flops 32000000000 | bytes 40000000 | tf_op jit(solution)/shard_map/pallas_call | solution.py:542
  186.6 0.0 copy-start.5
  186.6 0.0 copy-start.7
  186.6 0.0 copy-start.8
  186.7 0.0 copy-start.6
  186.7 0.0 collective-permute-done.3.refs_1_
  186.7 0.0 copy-start
  186.7 0.0 collective-permute-done.4.refs_2_
  186.7 0.0 collective-permute-done.5.refs_3_
  186.7 71.2 %shard_map.602 = (bf16[1184,16,128]{2,1,0:T(8,128)(2,1)}, f32[16,512]{1,0:T(8,128)}) custom-call(bf16[1184,16,128]{2,1,0:T(8,128)(2,1)} %get-tuple-element.165.own_ref, f32[16,512]{1,0:T(8,128)} %get-tuple-element.166.small_ref), custom_call_target="tpu_custom_call" | custom-call | flops 10000000 | bytes 200000000 | tf_op jit(solution)/shard_map/pallas_call | solution.py:998
  257.9 0.4 collective-permute-start.9
  258.4 1.3 collective-permute-start.10
  259.7 0.2 collective-permute-start.11
  259.9 0.7 reshape.192.vector_refs_2_
  260.6 0.6 reshape.185.line_refs_0__1_
  261.2 0.6 reshape.189.line_refs_2__1_
  261.8 0.0 copy-done.8
  261.8 0.6 reshape.191.line_refs_3__1_
  262.4 0.7 reshape.193.moment_refs_2_
  263.0 21.8 %shard_map.604 = (f32[1,1]{1,0:T(1,128)}, f32[432,1296]{1,0:T(8,128)}, f32[432,432]{1,0:T(8,128)}, f32[432,1728]{1,0:T(8,128)}, f32[432,1728]{1,0:T(8,128)}, /*i...) custom-call(bf16[1184,16,128]{2,1,0:T(8,128)(2,1)} %get-tuple-elemen, ...), custom_call_target="tpu_custom_call" | custom-call | tf_op jit(solution)/shard_map/pallas_call | solution.py:1231
  284.9 1.4 reshape.195
  286.3 1.4 reshape.196
  287.6 1.3 reduce
  288.9 1.3 reduce.1
  290.3 1.3 reduce.2
  291.6 1.4 reshape.205
  292.9 0.0 collective-permute-done.9.refs_5_
  292.9 0.0 collective-permute-done.10.refs_6_
  293.0 1.4 collective-permute-done.11.refs_7_
  294.3 16.2 %shard_map.603 = (bf16[100,32,432]{2,1,0:T(8,128)(2,1)}, f32[100,32,432]{2,1,0:T(8,128)}) custom-call(s32[32]{0:T(128)} %get-tuple-element.206.order_ref, s32[32]{0:T(128)} %fusion.2.class_ref, s32[1]{0:T(128)} %bitcast.band_ref, bf16[3,100,96]{2,1,0:T(8,128)(2,1)} %constant.85.clone.table_ref, bf16[2,4,96,432]{3,2,1,0:T(8,128)(2,1)} %get-tuple-element.157.refs_0_, ...), custom_call_target="tpu_custom_call" | custom-call | flops 10000000 | bytes 16000000 | tf_op jit(solution)/shard_map/pallas_call | solution.py:656
  (16 shorter events, 0.1 us)
Async XLA Ops:
  3.5 12.6 %copy-start.4 = (f32[1728]{0:T(1024)S(1)}, f32[1728]{0:T(1024)}, u32[]{:S(2)}) copy-start(f32[1728]{0:T(1024)} %param.47) | copy-start | bytes 20740
  12.9 30.7 %collective-permute-start = (bf16[2,4,96,432]{3,2,1,0:T(8,128)(2,1)}, bf16[2,4,96,432]{3,2,1,0:T(8,128)(2,1)S(1)}, u32[]{:S(2)}, u32[]{:S(2)}) collective-permute-start(bf16[2,4,96,432]{3,2,1,0:T(8,128)(2,1)} %get-tuple-element.128), channel_id=1, source_target_pairs={{0,1},{1,0},{2,3},{3,2},{4,5},{5,4},{6,7},{7,6},{8,9},{9,8},{10,11... | collective-permute-start | bytes 1990664 | tf_op jit(solution)/shard_map/ppermute | solution.py:1320
  13.3 30.2 %collective-permute-start.1 = (bf16[2,4,96,432]{3,2,1,0:T(8,128)(2,1)}, bf16[2,4,96,432]{3,2,1,0:T(8,128)(2,1)S(1)}, u32[]{:S(2)}, u32[]{:S(2)}) collective-permute-start(bf16[2,4,96,432]{3,2,1,0:T(8,128)(2,1)} %get-tuple-element.129), channel_id=1, source_target_pairs={{0,2},{1,3},{2,0},{3,1},{4,6},{5,7},{6,4},{7,5},{8,10},{9,11},{10,... | collective-permute-start | bytes 1990664 | tf_op jit(solution)/shard_map/ppermute | solution.py:1320
  15.8 35.1 %collective-permute-start.2 = (bf16[2,4,96,432]{3,2,1,0:T(8,128)(2,1)}, bf16[2,4,96,432]{3,2,1,0:T(8,128)(2,1)S(1)}, u32[]{:S(2)}, u32[]{:S(2)}) collective-permute-start(bf16[2,4,96,432]{3,2,1,0:T(8,128)(2,1)} %get-tuple-element.130), channel_id=1, source_target_pairs={{0,3},{1,2},{2,1},{3,0},{4,7},{5,6},{6,5},{7,4},{8,11},{9,10},{10,... | collective-permute-start | bytes 1990664 | tf_op jit(solution)/shard_map/ppermute | solution.py:1320
  27.2 25.5 %copy-start.10 = (bf16[2,4,96,432]{3,2,1,0:T(8,128)(2,1)S(1)}, bf16[2,4,96,432]{3,2,1,0:T(8,128)(2,1)}, u32[]{:S(2)}) copy-start(bf16[2,4,96,432]{3,2,1,0:T(8,128)(2,1)} %get-tuple-element.153) | copy-start | bytes 1990660
  43.6 10.4 %copy-start.9 = (bf16[2,4,96,432]{3,2,1,0:T(8,128)(2,1)}, bf16[2,4,96,432]{3,2,1,0:T(8,128)(2,1)S(1)}, u32[]{:S(2)}) copy-start(bf16[2,4,96,432]{3,2,1,0:T(8,128)(2,1)S(1)} %collective-permute-done.xct_refs_1_) | copy-start | bytes 1990660
  43.6 10.4 %copy-start.11 = (bf16[2,4,96,432]{3,2,1,0:T(8,128)(2,1)}, bf16[2,4,96,432]{3,2,1,0:T(8,128)(2,1)S(1)}, u32[]{:S(2)}) copy-start(bf16[2,4,96,432]{3,2,1,0:T(8,128)(2,1)S(1)} %collective-permute-done.1.xct_refs_2_) | copy-start | bytes 1990660
  50.9 3.1 copy-start.12
  50.9 91.0 %collective-permute-start.6 = (bf16[2,4,96,432]{3,2,1,0:T(8,128)(2,1)}, bf16[2,4,96,432]{3,2,1,0:T(8,128)(2,1)}, u32[]{:S(2)}, u32[]{:S(2)}) collective-permute-start(bf16[2,4,96,432]{3,2,1,0:T(8,128)(2,1)} %get-tuple-element.151), channel_id=1, source_target_pairs={{0,1},{1,0},{2,3},{3,2},{4,5},{5,4},{6,7},{7,6},{8,9},{9,8},{10,11... | collective-permute-start | bytes 1990664 | tf_op jit(solution)/shard_map/ppermute | solution.py:1320
  51.0 91.1 %collective-permute-start.7 = (bf16[2,4,96,432]{3,2,1,0:T(8,128)(2,1)}, bf16[2,4,96,432]{3,2,1,0:T(8,128)(2,1)}, u32[]{:S(2)}, u32[]{:S(2)}) collective-permute-start(bf16[2,4,96,432]{3,2,1,0:T(8,128)(2,1)} %get-tuple-element.152), channel_id=1, source_target_pairs={{0,2},{1,3},{2,0},{3,1},{4,6},{5,7},{6,4},{7,5},{8,10},{9,11},{10,... | collective-permute-start | bytes 1990664 | tf_op jit(solution)/shard_map/ppermute | solution.py:1320
  52.7 89.5 %collective-permute-start.8 = (bf16[2,4,96,432]{3,2,1,0:T(8,128)(2,1)S(1)}, bf16[2,4,96,432]{3,2,1,0:T(8,128)(2,1)}, u32[]{:S(2)}, u32[]{:S(2)}) collective-permute-start(bf16[2,4,96,432]{3,2,1,0:T(8,128)(2,1)S(1)} %copy-done.10), channel_id=1, source_target_pairs={{0,3},{1,2},{2,1},{3,0},{4,7},{5,6},{6,5},{7,4},{8,11},{9,10},{10,... | collective-permute-start | bytes 1990664 | tf_op jit(solution)/shard_map/ppermute | solution.py:1320
  140.2 46.5 %collective-permute-start.3 = (bf16[2,4,96,432]{3,2,1,0:T(8,128)(2,1)}, bf16[2,4,96,432]{3,2,1,0:T(8,128)(2,1)S(1)}, u32[]{:S(2)}, u32[]{:S(2)}) collective-permute-start(bf16[2,4,96,432]{3,2,1,0:T(8,128)(2,1)} %get-tuple-element.147), channel_id=1, source_target_pairs={{0,1},{1,0},{2,3},{3,2},{4,5},{5,4},{6,7},{7,6},{8,9},{9,8},{10,11... | collective-permute-start | bytes 1990664 | tf_op jit(solution)/shard_map/ppermute | solution.py:1320
  140.7 46.0 %collective-permute-start.4 = (bf16[2,4,96,432]{3,2,1,0:T(8,128)(2,1)}, bf16[2,4,96,432]{3,2,1,0:T(8,128)(2,1)S(1)}, u32[]{:S(2)}, u32[]{:S(2)}) collective-permute-start(bf16[2,4,96,432]{3,2,1,0:T(8,128)(2,1)} %get-tuple-element.148), channel_id=1, source_target_pairs={{0,2},{1,3},{2,0},{3,1},{4,6},{5,7},{6,4},{7,5},{8,10},{9,11},{10,... | collective-permute-start | bytes 1990664 | tf_op jit(solution)/shard_map/ppermute | solution.py:1320
  141.9 44.8 %collective-permute-start.5 = (bf16[2,4,96,432]{3,2,1,0:T(8,128)(2,1)}, bf16[2,4,96,432]{3,2,1,0:T(8,128)(2,1)S(1)}, u32[]{:S(2)}, u32[]{:S(2)}) collective-permute-start(bf16[2,4,96,432]{3,2,1,0:T(8,128)(2,1)} %get-tuple-element.149), channel_id=1, source_target_pairs={{0,3},{1,2},{2,1},{3,0},{4,7},{5,6},{6,5},{7,4},{8,11},{9,10},{10,... | collective-permute-start | bytes 1990664 | tf_op jit(solution)/shard_map/ppermute | solution.py:1320
  186.6 73.9 %copy-start.5 = (f32[1296]{0:T(1024)S(1)}, f32[1296]{0:T(1024)}, u32[]{:S(2)}) copy-start(f32[1296]{0:T(1024)} %param.50) | copy-start | bytes 15556
  186.6 74.5 %copy-start.7 = (f32[1728]{0:T(1024)S(1)}, f32[1728]{0:T(1024)}, u32[]{:S(2)}) copy-start(f32[1728]{0:T(1024)} %param.54) | copy-start | bytes 20740
  186.6 75.1 %copy-start.8 = (f32[1728]{0:T(1024)S(1)}, f32[1728]{0:T(1024)}, u32[]{:S(2)}) copy-start(f32[1728]{0:T(1024)} %param.55) | copy-start | bytes 20740
  186.7 75.7 %copy-start.6 = (f32[1728]{0:T(1024)S(1)}, f32[1728]{0:T(1024)}, u32[]{:S(2)}) copy-start(f32[1728]{0:T(1024)} %param.59) | copy-start | bytes 20740
  186.7 98.2 %copy-start = (bf16[2,4,96,432]{3,2,1,0:T(8,128)(2,1)}, bf16[2,4,96,432]{3,2,1,0:T(8,128)(2,1)S(1)}, u32[]{:S(2)}) copy-start(bf16[2,4,96,432]{3,2,1,0:T(8,128)(2,1)S(1)} %collective-permute-done.3.refs_1_) | copy-start | bytes 1990660
  186.7 98.2 %copy-start.1 = (bf16[2,4,96,432]{3,2,1,0:T(8,128)(2,1)}, bf16[2,4,96,432]{3,2,1,0:T(8,128)(2,1)S(1)}, u32[]{:S(2)}) copy-start(bf16[2,4,96,432]{3,2,1,0:T(8,128)(2,1)S(1)} %collective-permute-done.4.refs_2_) | copy-start | bytes 1990660
  186.7 98.2 %copy-start.2 = (bf16[2,4,96,432]{3,2,1,0:T(8,128)(2,1)}, bf16[2,4,96,432]{3,2,1,0:T(8,128)(2,1)S(1)}, u32[]{:S(2)}) copy-start(bf16[2,4,96,432]{3,2,1,0:T(8,128)(2,1)S(1)} %collective-permute-done.5.refs_3_) | copy-start | bytes 1990660
  257.9 35.0 %collective-permute-start.9 = (bf16[2,4,96,432]{3,2,1,0:T(8,128)(2,1)}, bf16[2,4,96,432]{3,2,1,0:T(8,128)(2,1)S(1)}, u32[]{:S(2)}, u32[]{:S(2)}) collective-permute-start(bf16[2,4,96,432]{3,2,1,0:T(8,128)(2,1)} %get-tuple-element.169), channel_id=1, source_target_pairs={{0,1},{1,0},{2,3},{3,2},{4,5},{5,4},{6,7},{7,6},{8,9},{9,8},{10,11... | collective-permute-start | bytes 1990664 | tf_op jit(solution)/shard_map/ppermute | solution.py:1320
  258.4 34.6 %collective-permute-start.10 = (bf16[2,4,96,432]{3,2,1,0:T(8,128)(2,1)}, bf16[2,4,96,432]{3,2,1,0:T(8,128)(2,1)}, u32[]{:S(2)}, u32[]{:S(2)}) collective-permute-start(bf16[2,4,96,432]{3,2,1,0:T(8,128)(2,1)} %get-tuple-element.170), channel_id=1, source_target_pairs={{0,2},{1,3},{2,0},{3,1},{4,6},{5,7},{6,4},{7,5},{8,10},{9,11},{10,... | collective-permute-start | bytes 1990664 | tf_op jit(solution)/shard_map/ppermute | solution.py:1320
  259.7 34.6 %collective-permute-start.11 = (bf16[2,4,96,432]{3,2,1,0:T(8,128)(2,1)}, bf16[2,4,96,432]{3,2,1,0:T(8,128)(2,1)}, u32[]{:S(2)}, u32[]{:S(2)}) collective-permute-start(bf16[2,4,96,432]{3,2,1,0:T(8,128)(2,1)} %get-tuple-element.171), channel_id=1, source_target_pairs={{0,3},{1,2},{2,1},{3,0},{4,7},{5,6},{6,5},{7,4},{8,11},{9,10},{10,... | collective-permute-start | bytes 1990664 | tf_op jit(solution)/shard_map/ppermute | solution.py:1320
  292.9 1.4 copy-start.3

commit v2 on v1

--- a/solution.py
+++ b/solution.py
@@ -26,12 +26,12 @@
 SUB = 16
 SMALL_ROWS = 16
 WAVES = (
-    ("cyxlh", 7, 0),
-    ("cxylh", 7, 0),
-    ("clhxy", 4, 0),
-    ("cyxlh", 7, 1),
-    ("cxylh", 7, 1),
-    ("clhxy", 5, 1),
+    ("cyxlh", 7),
+    ("cxylh", 7),
+    ("clhxy", 4),
+    ("cyxlh", 7),
+    ("cxylh", 7),
+    ("clhxy", 5),
 )
 LANE = 128
 
@@ -72,6 +72,32 @@
     made = select_matrix(side, bands).reshape(-1, bands, piece_rows(bands))
     ordered = [made[:, [own ^ step for step in range(bands)]] for own in range(bands)]
     return np.stack(ordered).reshape(bands, made.shape[0], -1)
+
+
+def rest_matrices(side, bands):
+    piece = piece_rows(bands)
+    made = select_matrices(side, bands).reshape(bands, -1, bands, piece)
+    halves = [made[..., : piece // 2], made[..., piece // 2 :]]
+    return np.stack([half.reshape(bands, made.shape[1], -1) for half in halves], axis=1)
+
+
+def stored_shape(piece, columns):
+    main = columns // LANE * LANE
+    return piece + piece // 2 * LANE // main, main
+
+
+def folded(ref, which, index, piece):
+    rows, main = ref.shape[2:]
+    pieces = [ref[which, index, piece:, low : low + LANE] for low in range(0, main, LANE)]
+    return jnp.concatenate(pieces, axis=0)
+
+
+def fold(ref, which, index, piece, block):
+    rows, main = ref.shape[2:]
+    each = rows - piece
+    for tile in range(main // LANE):
+        at = slice(tile * LANE, (tile + 1) * LANE)
+        ref[which, index, piece:, at] = block[tile * each : (tile + 1) * each]
 
 
 def pack_matrix(bands):
@@ -103,6 +129,8 @@
     small_in,
     sel_refs,
     selt_refs,
+    rest_refs,
+    restt_refs,
     place_hbm,
     moment_refs,
     weight_hbm,
@@ -130,8 +158,12 @@
     g1_ref,
     g2t_ref,
     gsum_refs,
-    gm_s,
-    gc_s,
+    gm_refs,
+    gc_refs,
+    second_s,
+    ct_s,
+    secondt_s,
+    ctt_s,
     place_refs,
     weight_refs,
     copy_sem,
@@ -194,32 +226,83 @@
         for ref in gsum_refs:
             ref[...] = jnp.zeros_like(ref)
 
+    def aligned(value, unit):
+        return value if isinstance(value, int) else pl.multiple_of(value, unit)
+
     def head_place(head):
         first_lane = head * head_size
-        start = min(first_lane // LANE * LANE, width - window)
+        if isinstance(head, int):
+            start = min(first_lane // LANE * LANE, width - window)
+        else:
+            start = jnp.minimum(first_lane // LANE * LANE, width - window)
         lanes = lax.broadcasted_iota(jnp.int32, (1, window), 1) + start
         mask = (lanes >= first_lane) & (lanes < first_lane + head_size)
-        return start, mask, first_lane
-
-    def skewed(*stages):
-        for index in range(heads + len(stages) - 1):
-            for late, stage in enumerate(stages):
-                if 0 <= index - late < heads:
-                    stage(index - late)
-
-    def image(side, sel_ref, selt_ref, place_ref, gsum_ref):
+        return start, mask
+
+    def part_lanes(part, start):
+        return pl.ds(aligned(part * width + start, LANE), window)
+
+    def head_rows(part, head):
+        return pl.ds(aligned(part * columns + head * head_size, SUB), head_size)
+
+    def skewed(compact, enter, middle, leave):
+        if not compact:
+            for index in range(heads + 2):
+                if index < heads:
+                    enter(index, index % 2)
+                if 1 <= index <= heads:
+                    middle(index - 1, (index - 1) % 2)
+                if index >= 2:
+                    leave(index - 2, index % 2)
+            return
+        enter(0, 0)
+
+        def pair(index, carry):
+            for odd in range(2):
+                head = index * 2 + odd
+                leave(jnp.maximum(head - 1, 0), 1 - odd)
+                enter(head + 1, 1 - odd)
+                middle(head, odd)
+            return carry
+
+        pairs = (heads - 1) // 2
+        lax.fori_loop(0, pairs, pair, 0)
+        for head in range(2 * pairs, heads):
+            leave(head - 1, (head - 1) % 2)
+            if head + 1 < heads:
+                enter(head + 1, (head + 1) % 2)
+            middle(head, head % 2)
+        leave(heads - 1, (heads - 1) % 2)
+
+    def image(side, sel_ref, selt_ref, rest_ref, restt_ref, place_ref, gsum_ref):
         live, rows, lanes = side_sizes(side)
         edge = live // 8 * 8
-        tall = outig_refs[0].shape[2]
+        compact = (side != SIDES[0]) != started
+        tall = sel_ref.shape[2] // len(xct_refs)
+        main = xct_refs[0].shape[3]
 
         def gathered(which):
-            pieces = jnp.concatenate([ref[which, 0] for ref in xct_refs], axis=0)
-            return dot_nn(sel_ref[0], pieces)
+            pieces = jnp.concatenate([ref[which, 0, :tall] for ref in xct_refs], axis=0)
+            blocks = [folded(ref, which, 0, tall) for ref in xct_refs]
+            block = jnp.concatenate(blocks, axis=0)
+            rest = dot_nn(rest_ref[0, 0], block)
+            rest += pltpu.roll(dot_nn(rest_ref[0, 1], block), LANE // 2, 1)
+            return jnp.concatenate(
+                [dot_nn(sel_ref[0], pieces), rest[:, : columns - main]], axis=1
+            )
 
         def spread(which, values):
-            values = dot_nn(selt_ref[0], values.astype(BF16)).astype(BF16)
+            values = values.astype(BF16)
+            fill = jnp.zeros((rows, LANE - (columns - main)), BF16)
+            rest = jnp.concatenate([values[:, main:], fill], axis=1)
+            values = dot_nn(selt_ref[0], values[:, :main]).astype(BF16)
+            block = dot_nn(restt_ref[0, 0], rest)
+            block += pltpu.roll(dot_nn(restt_ref[0, 1], rest), LANE // 2, 1)
+            block = block.astype(BF16)
             for index, ref in enumerate(outig_refs):
-                ref[which, 0] = values[index * tall : (index + 1) * tall]
+                ref[which, 0, :tall] = values[index * tall : (index + 1) * tall]
+                half = tall // 2
+                fold(ref, which, 0, tall, block[index * half : (index + 1) * half])
 
         def norm(values):
             averaged = jnp.mean(values, axis=-1, keepdims=True)
@@ -246,32 +329,38 @@
             piece = proj_s[:lanes, part * width : (part + 1) * width]
             projt_s[part, :, :lanes] = piece.T
 
-        def score_head(head):
-            start, mask, row = head_place(head)
-            query = jnp.where(mask, proj_s[:lanes, start : start + window], 0)
-            key = proj_s[:rows, width + start : width + start + window]
-            cont_s[head, :rows, :lanes] = dot_nt(key, query)
-
-        def soft_head(head):
-            score = cont_s[head, :rows, :lanes] * (score_scale * math.log2(math.e))
+        tops = {}
+
+        def score_head(head, slot):
+            start, mask = head_place(head)
+            query = jnp.where(mask, proj_s[:lanes, part_lanes(0, start)], 0)
+            key = proj_s[:rows, part_lanes(1, start)]
+            score = dot_nt(key, query)
             tail = lax.broadcasted_iota(jnp.int32, (rows - edge, lanes), 0) < live - edge
             score = jnp.concatenate(
                 [score[:edge], jnp.where(tail, score[edge:], MASKED)], axis=0
             )
-            top = jnp.max(score, axis=0, keepdims=True)
-            raised = jnp.exp2(score - top)
+            gm_refs[slot][:rows, :lanes] = score
+            if not compact:
+                tops[head] = jnp.max(score, axis=0, keepdims=True)
+
+        def soft_head(head, slot):
+            factor = score_scale * math.log2(math.e)
+            score = gm_refs[slot][:rows, :lanes]
+            top = jnp.max(score, axis=0, keepdims=True) if compact else tops[head]
+            raised = jnp.exp2(score * factor - top * factor)
             total = jnp.sum(raised, axis=0, keepdims=True)
             content = raised * (gate_ref[head] / total)
             cont_s[head, :rows, :lanes] = content
             mix_s[head, :rows, :lanes] = (content + place_ref[head]).astype(BF16)
 
-        def attend_head(head):
-            row = head * head_size
-            value_t = projt_s[2, row : row + head_size, :rows]
+        def attend_head(head, slot):
+            here = head_rows(0, head)
+            value_t = projt_s[2, here, :rows]
             mixed = mix_s[head, :rows, :lanes]
-            attt_s[row : row + head_size, :lanes] = dot_nn(value_t, mixed).astype(BF16)
-
-        skewed(score_head, soft_head, attend_head)
+            attt_s[here, :lanes] = dot_nn(value_t, mixed).astype(BF16)
+
+        skewed(compact, score_head, soft_head, attend_head)
 
         once(load_out, load_w1, load_w2, load_back)
         attended = attt_s[:, :lanes].T[:rows]
@@ -280,10 +369,13 @@
         second_b = (unit_two * gains_ref[1:2, :] + biases_ref[1:2, :]).astype(BF16)
         ct_b = gathered(1).astype(BF16)
 
-        for index in range(chunks):
-            at = slice(index * chunk, (index + 1) * chunk)
-            before = dot_nn(second_b, w1_ref[:, at]) + fc1b_ref[:, at]
-            grad_act = dot_nn(ct_b, w2t_ref[:, at])
+        second_s[:rows, :] = second_b
+        ct_s[:rows, :] = ct_b
+
+        def mlp_chunk(index):
+            at = pl.ds(aligned(index * chunk, chunk), chunk)
+            before = dot_nn(second_s[:rows, :], w1_ref[:, at]) + fc1b_ref[:, at]
+            grad_act = dot_nn(ct_s[:rows, :], w2t_ref[:, at])
             square = before * before
             inner = before * (
                 math.sqrt(2.0 / math.pi) + (math.sqrt(2.0 / math.pi) * 0.044715) * square
@@ -299,18 +391,38 @@
             gb_s[:rows, at] = grad_b
             fc1g_s[:, at] += fold_rows(grad_b.astype(F32))
 
+        def weight_chunk(index):
+            at = pl.ds(aligned(index * chunk, chunk), chunk)
+            g1_ref[:, at] += dot_nn(secondt_s[:, :rows], gb_s[:rows, at])
+            g2t_ref[:, at] += dot_nn(ctt_s[:, :rows], act_s[:rows, at])
+
+        def mlp_step(index, carry):
+            weight_chunk(index - 1)
+            mlp_chunk(index)
+            return carry
+
+        if compact:
+            ctt_s[:, :rows] = ct_b.T
+            secondt_s[:, :rows] = second_b.T
+            mlp_chunk(0)
+            lax.fori_loop(1, chunks, mlp_step, 0)
+            weight_chunk(chunks - 1)
+        else:
+            for index in range(chunks):
+                mlp_chunk(index)
+
         result = (
             hidden + dot_nt(act_s[:rows, :], w2t_ref[...]) + biases_ref[3:4, :]
         )
         spread(0, result)
 
-        ct_t = ct_b.T
-        second_t = second_b.T
-        units = hidden_units
-        for index in range(chunks):
-            low, high = index * chunk, min((index + 1) * chunk, units)
-            g1_ref[:, low:high] += dot_nn(second_t, gb_s[:rows, low:high])
-            g2t_ref[:, low:high] += dot_nn(ct_t, act_s[:rows, low:high])
+        if not compact:
+            ct_t = ct_b.T
+            second_t = second_b.T
+            for index in range(chunks):
+                low, high = index * chunk, min((index + 1) * chunk, hidden_units)
+                g1_ref[:, low:high] += dot_nn(second_t, gb_s[:rows, low:high])
+                g2t_ref[:, low:high] += dot_nn(ct_t, act_s[:rows, low:high])
 
         ct_f = ct_b.astype(F32)
         grad_second = dot_nt(gb_s[:rows, :], w1_ref[...])
@@ -326,37 +438,42 @@
             da_s[rows:lanes, :] = jnp.zeros((lanes - rows, width), BF16)
         dat_s[:, :lanes] = da_s[:lanes, :].T
 
-        def grad_head(head):
-            start, mask, row = head_place(head)
-            grad_att = jnp.where(mask, da_s[:lanes, start : start + window], 0)
-            value = proj_s[:rows, 2 * width + start : 2 * width + start + window]
-            gm_s[head % 2, :rows, :lanes] = dot_nt(value, grad_att)
-
-        def soft_back_head(head):
-            grad_mixed = gm_s[head % 2, :rows, :lanes]
+        totals = {}
+
+        def grad_head(head, slot):
+            start, mask = head_place(head)
+            grad_att = jnp.where(mask, da_s[:lanes, part_lanes(0, start)], 0)
+            value = proj_s[:rows, part_lanes(2, start)]
+            grad_mixed = dot_nt(value, grad_att)
             gsum_ref[head] += grad_mixed
+            product = grad_mixed * cont_s[head, :rows, :lanes]
+            gm_refs[slot][:rows, :lanes] = product
+            if not compact:
+                totals[head] = jnp.sum(product, axis=0, keepdims=True) / gate_ref[head]
+
+        def soft_back_head(head, slot):
+            product = gm_refs[slot][:rows, :lanes]
+            if compact:
+                total = jnp.sum(product, axis=0, keepdims=True) / gate_ref[head]
+            else:
+                total = totals[head]
+            racc_s[SIDES.index(side), head, :, :lanes] += total
             content = cont_s[head, :rows, :lanes]
-            product = grad_mixed * content
-            total = jnp.sum(product, axis=0, keepdims=True) / gate_ref[head]
-            racc_s[SIDES.index(side), head, :, :lanes] += total
-            gc_s[head % 2, :rows, :lanes] = (product - content * total).astype(BF16)
-
-        def back_head(head):
-            row = head * head_size
-            here = slice(row, row + head_size)
+            gc_refs[slot][:rows, :lanes] = (product - content * total).astype(BF16)
+
+        def back_head(head, slot):
+            here = head_rows(0, head)
             mixed = mix_s[head, :rows, :lanes]
-            grad_content = gc_s[head % 2, :rows, :lanes]
-            gt_s[2 * columns + row : 2 * columns + row + head_size, :rows] = dot_nt(
-                dat_s[here, :lanes], mixed
-            ).astype(BF16)
-            gt_s[columns + row : columns + row + head_size, :rows] = (
+            grad_content = gc_refs[slot][:rows, :lanes]
+            gt_s[head_rows(2, head), :rows] = dot_nt(dat_s[here, :lanes], mixed).astype(BF16)
+            gt_s[head_rows(1, head), :rows] = (
                 dot_nt(projt_s[0, here, :lanes], grad_content) * score_scale
             ).astype(BF16)
             gt_s[here, :lanes] = (
                 dot_nn(projt_s[1, here, :rows], grad_content) * score_scale
             ).astype(BF16)
 
-        skewed(grad_head, soft_back_head, back_head)
+        skewed(compact, grad_head, soft_back_head, back_head)
 
         first_t = first_b.T
         grad_proj = gt_s[:, :lanes].T[:rows]
@@ -371,7 +488,15 @@
 
         @pl.when(sizes_ref[step] == side)
         def _(index=index, side=side):
-            image(side, sel_refs[index], selt_refs[index], place_refs[index], gsum_refs[index])
+            image(
+                side,
+                sel_refs[index],
+                selt_refs[index],
+                rest_refs[index],
+                restt_refs[index],
+                place_refs[index],
+                gsum_refs[index],
+            )
 
     @pl.when(step == steps - 1)
     def _():
@@ -463,9 +588,14 @@
             small_ref[...] += small_in[...]
 
 
+def matrices_columns(shared):
+    return shared[3][0].shape[0]
+
+
 def run_images(xct, sizes, start, band, shared, previous, units, tile_count):
     bands = len(xct)
-    _, images, piece, columns = xct[0].shape
+    _, images, stored, main = xct[0].shape
+    columns = matrices_columns(shared)
     places, moments, gate_open, matrices, gains, biases, fc1b = shared
     heads = gate_open.shape[0]
     width = matrices[0].shape[1] // 3
@@ -473,6 +603,9 @@
     chosen = [select_matrices(side, bands) for side in SIDES]
     sels = [jnp.asarray(made, BF16) for made in chosen]
     selts = [jnp.asarray(made.transpose(0, 2, 1), BF16) for made in chosen]
+    chosen = [rest_matrices(side, bands) for side in SIDES]
+    rests = [jnp.asarray(made, BF16) for made in chosen]
+    restts = [jnp.asarray(made.transpose(0, 1, 3, 2), BF16) for made in chosen]
     sizes_all = [side_sizes(side) for side in SIDES]
     most_rows = max(size[1] for size in sizes_all)
     most_lanes = max(size[2] for size in sizes_all)
@@ -487,11 +620,11 @@
     def own(array):
         return pl.BlockSpec(
             (1,) + array.shape[1:],
-            lambda i, sizes, band, *_: (band[0], 0, 0),
+            lambda i, sizes, band, *_: (band[0],) + (0,) * (array.ndim - 1),
             pipeline_mode=pl.Buffered(1),
         )
 
-    image_specs = [pl.BlockSpec((2, 1, piece, columns), lambda i, *_: (0, i, 0, 0))] * bands
+    image_specs = [pl.BlockSpec((2, 1, stored, main), lambda i, *_: (0, i, 0, 0))] * bands
     out_shapes = [
         [jax.ShapeDtypeStruct(part.shape, BF16) for part in xct],
         jax.ShapeDtypeStruct((tile_count, SUB, LANE), BF16),
@@ -518,13 +651,17 @@
         pltpu.VMEM((columns, padded), F32),
         pltpu.VMEM((columns, padded), F32),
         [pltpu.VMEM((heads, size[1], size[2]), F32) for size in sizes_all],
-        pltpu.VMEM((2, most_rows, most_lanes), F32),
-        pltpu.VMEM((2, most_rows, most_lanes), BF16),
+        [pltpu.VMEM((most_rows, most_lanes), F32)] * 2,
+        [pltpu.VMEM((most_rows, most_lanes), BF16)] * 2,
+        pltpu.VMEM((most_rows, columns), BF16),
+        pltpu.VMEM((most_rows, columns), BF16),
+        pltpu.VMEM((columns, most_lanes), BF16),
+        pltpu.VMEM((columns, most_lanes), BF16),
         [pltpu.VMEM(place.shape, F32) for place in places],
         [pltpu.VMEM(matrix.shape, BF16) for matrix in matrices],
         pltpu.SemaphoreType.DMA((1 + len(places) + len(matrices),)),
     ]
-    smalls = [sels, selts, list(places), list(moments), list(matrices), gains, biases, fc1b]
+    smalls = [sels, selts, rests, restts, list(places), list(moments), list(matrices), gains, biases, fc1b]
     body = functools.partial(image_kernel, columns, heads, units, images, started)
     hbm = lambda _: pl.BlockSpec(memory_space=pl.ANY)
     specs = [
@@ -532,6 +669,8 @@
         whole(previous[1]),
         jax.tree.map(own, sels),
         jax.tree.map(own, selts),
+        jax.tree.map(own, rests),
+        jax.tree.map(own, restts),
         [hbm(None) for _ in places],
         jax.tree.map(whole, list(moments)),
         [hbm(None) for _ in matrices],
@@ -563,16 +702,41 @@
     ]
 
 
+def loop_rows(rows, count, body, after=None):
+    def step(index, carry):
+        for row in range(8):
+            start = pl.multiple_of(index * (8 * (count + 1)), 8) + row * (count + 1)
+            body(index * 8 + row, pl.ds(start, count))
+        if after is not None:
+            after(pl.ds(index * 8, 8))
+        return carry
+
+    lax.fori_loop(0, rows // 8, step, 0)
+    for row in range(rows // 8 * 8, rows):
+        body(row, pl.ds(row * (count + 1), count))
+    if after is not None and rows % 8:
+        after(pl.ds(rows // 8 * 8, rows % 8))
+
+
 def pack_kernel(first, order_ref, class_ref, band_ref, x_ref, ct_ref, table_ref, *refs):
-    outs, wides = refs[:-2], refs[-2:]
+    outs, wides, held, copy_sem = refs[:-4], refs[-4:-2], refs[-2], refs[-1]
     rows, count, columns = x_ref.shape
     images = count // len(outs)
-
-    for source, wide in zip((x_ref, ct_ref), wides):
-        for row in range(rows):
-            for index, low, high in lane_tiles(columns):
-                at = slice(row * (count + 1), row * (count + 1) + count)
-                wide[index, at, : high - low] = source[row, :, low:high].astype(F32)
+    loads = [
+        pltpu.make_async_copy(source, held.at[index], copy_sem.at[index])
+        for index, source in enumerate((x_ref, ct_ref))
+    ]
+    for load in loads:
+        load.start()
+
+    for load, index, wide in zip(loads, range(2), wides):
+        load.wait()
+
+        def widen(row, at, index=index, wide=wide):
+            for tile, low, high in lane_tiles(columns):
+                wide[tile, at, : high - low] = held[index, row, :, low:high].astype(F32)
+
+        loop_rows(rows, count, widen)
 
     for step, out in enumerate(outs):
 
@@ -580,13 +744,20 @@
             place = (band_ref[0] ^ step) * images + first + index
             at = pl.ds(order_ref[place], rows, stride=count + 1)
             select = table_ref[class_ref[place]]
+            piece = table_ref.shape[1]
+            low_lanes = lax.broadcasted_iota(jnp.int32, (piece // 2, LANE), 1) < LANE // 2
             for which, wide in enumerate(wides):
                 for tile, low, high in lane_tiles(columns):
-                    taken = dot_nn(select, wide[tile, at, :].astype(BF16)).astype(BF16)
-                    out[which, index, :, low:high] = taken[:, : high - low]
+                    taken = dot_nn(select, wide[tile, at, :].astype(BF16))
+                    if high - low == LANE:
+                        out[which, index, :piece, low:high] = taken.astype(BF16)
+                    else:
+                        upper = pltpu.roll(taken[piece // 2 :], LANE // 2, 1)
+                        block = jnp.where(low_lanes, taken[: piece // 2], upper)
+                        fold(out, which, index, piece, block.astype(BF16))
             return carry
 
-        lax.fori_loop(0, out.shape[1], one, 0)
+        lax.fori_loop(0, out.shape[1], one, 0, unroll=2)
 
 
 def pack_images(x, ct, order, classes, band, bands, first, size):
@@ -599,25 +770,29 @@
         grid_spec=pltpu.PrefetchScalarGridSpec(
             num_scalar_prefetch=3,
             grid=(),
-            in_specs=[vmem] * 3,
+            in_specs=[pl.BlockSpec(memory_space=pl.ANY)] * 2 + [vmem],
             out_specs=[vmem] * bands,
             scratch_shapes=[
                 pltpu.VMEM(
-                    (round_up(columns, LANE) // LANE, round_up(rows * (count + 1), 8), LANE), F32
+                    (round_up(columns, LANE) // LANE, round_up(rows, 8) * (count + 1), LANE), F32
                 )
             ]
-            * 2,
+            * 2
+            + [pltpu.VMEM((2, rows, count, columns), BF16), pltpu.SemaphoreType.DMA((2,))],
         ),
-        out_shape=[jax.ShapeDtypeStruct((2, size, piece, columns), BF16)] * bands,
+        out_shape=[jax.ShapeDtypeStruct((2, size) + stored_shape(piece, columns), BF16)] * bands,
         compiler_params=pltpu.CompilerParams(vmem_limit_bytes=VMEM_LIMIT),
         cost_estimate=pl.CostEstimate(flops=10_000_000, bytes_accessed=10_000_000, transcendentals=0),
     )(order, classes, band, x, ct, table)
 
 
-def unpack_kernel(chunks, bands, order_ref, class_ref, band_ref, table_ref, *refs):
-    parts, (out_ref, ig_ref), wides = refs[:-4], refs[-4:-2], refs[-2:]
+def unpack_kernel(
+    chunks, bands, order_ref, class_ref, band_ref, table_ref, low_ref, high_ref, *refs
+):
+    parts, targets, wides, held, copy_sem = refs[:-7], refs[-7:-5], refs[-5:-3], refs[-3:-1], refs[-1]
     images = sum(chunks)
-    rows, count, columns = out_ref.shape
+    rows, count, columns = targets[0].shape
+    piece = table_ref.shape[2]
     first = 0
     for chunk, size in enumerate(chunks):
         for step in range(bands):
@@ -626,54 +801,67 @@
             def one(index, carry, part=part, first=first, step=step):
                 place = (band_ref[0] ^ step) * images + first + index
                 at = pl.ds(order_ref[place], rows, stride=count + 1)
-                spread = table_ref[class_ref[place]]
+                kind = class_ref[place]
                 for which, wide in enumerate(wides):
                     for tile, low, high in lane_tiles(columns):
-                        made = dot_nn(spread, part[which, index, :, low:high])
-                        if high - low < LANE:
-                            fill = jnp.zeros((rows, LANE - (high - low)), F32)
-                            made = jnp.concatenate([made, fill], axis=1)
+                        if high - low == LANE:
+                            made = dot_nn(table_ref[kind], part[which, index, :piece, low:high])
+                        else:
+                            rest = folded(part, which, index, piece)
+                            made = dot_nn(low_ref[kind], rest)
+                            made += pltpu.roll(dot_nn(high_ref[kind], rest), LANE // 2, 1)
                         wide[tile, at, :] = made
                 return carry
 
-            lax.fori_loop(0, size, one, 0)
+            lax.fori_loop(0, size, one, 0, unroll=2)
         first += size
 
-    for target, wide in zip((out_ref, ig_ref), wides):
-        for row in range(rows):
+    for index, wide in enumerate(wides):
+
+        def narrow(row, at, index=index, wide=wide):
             for tile, low, high in lane_tiles(columns):
-                at = slice(row * (count + 1), row * (count + 1) + count)
-                target[row, :, low:high] = wide[tile, at, : high - low].astype(target.dtype)
-
-
-def unpack_images(parts, order, classes, band, chunks, rows):
+                values = wide[tile, at, : high - low]
+                held[index][row, :, low:high] = values.astype(held[index].dtype)
+
+        def leave(at, index=index):
+            pltpu.make_async_copy(
+                held[index].at[at], targets[index].at[at], copy_sem.at[index]
+            ).start()
+
+        loop_rows(rows, count, narrow, leave)
+    for index in range(2):
+        pltpu.make_async_copy(held[index], targets[index], copy_sem.at[index]).wait()
+
+
+def unpack_images(parts, order, classes, band, chunks, rows, columns):
     bands = len(parts[0])
-    columns = parts[0][0].shape[-1]
     count = bands * sum(chunks)
-    table = jnp.asarray(pack_matrix(bands).transpose(0, 2, 1), BF16)
+    made = pack_matrix(bands).transpose(0, 2, 1)
+    half = made.shape[2] // 2
+    tables = [jnp.asarray(t, BF16) for t in (made, made[..., :half], made[..., half:])]
     vmem = pl.BlockSpec(memory_space=pltpu.VMEM)
     flat = [piece for part in parts for piece in part]
+    shape = (rows, count, columns)
+    wide = (round_up(columns, LANE) // LANE, round_up(rows, 8) * (count + 1), LANE)
     return pl.pallas_call(
         functools.partial(unpack_kernel, chunks, bands),
         grid_spec=pltpu.PrefetchScalarGridSpec(
             num_scalar_prefetch=3,
             grid=(),
-            in_specs=[vmem] * (1 + len(flat)),
-            out_specs=[vmem] * 2,
+            in_specs=[vmem] * (3 + len(flat)),
+            out_specs=[pl.BlockSpec(memory_space=pl.ANY)] * 2,
             scratch_shapes=[
-                pltpu.VMEM(
-                    (round_up(columns, LANE) // LANE, round_up(rows * (count + 1), 8), LANE), F32
-                )
-            ]
-            * 2,
+                pltpu.VMEM(wide, F32),
+                pltpu.VMEM(wide, F32),
+                pltpu.VMEM(shape, BF16),
+                pltpu.VMEM(shape, F32),
+                pltpu.SemaphoreType.DMA((2,)),
+            ],
         ),
-        out_shape=[
-            jax.ShapeDtypeStruct((rows, count, columns), BF16),
-            jax.ShapeDtypeStruct((rows, count, columns), F32),
-        ],
+        out_shape=[jax.ShapeDtypeStruct(shape, BF16), jax.ShapeDtypeStruct(shape, F32)],
         compiler_params=pltpu.CompilerParams(vmem_limit_bytes=VMEM_LIMIT),
         cost_estimate=pl.CostEstimate(flops=10_000_000, bytes_accessed=16_000_000, transcendentals=0),
-    )(order, classes, band, table, *flat)
+    )(order, classes, band, *tables, *flat)
 
 
 def prep_kernel(head_ref, gate_ref, wqkv_in, wout_in, w1_in, w2t_in, *refs):
@@ -761,11 +949,11 @@
     weight = sum(wave[1] for wave in WAVES)
     waves = []
     base = before = taken = 0
-    for order, part, start in WAVES:
+    for order, part in WAVES:
         before += part
         share = -(-each * before // weight) - taken
         if share:
-            waves.append((base, share, order, start))
+            waves.append((base, share, order))
             base += devices * share
             taken += share
     return waves, each * devices
@@ -815,7 +1003,7 @@
         devices *= axes[name][1]
 
     loads = []
-    for w, (base, share, _, _) in enumerate(waves):
+    for w, (base, share, _) in enumerate(waves):
         at = pl.ds(base, devices * share)
         loads.append(pltpu.make_async_copy(own_ref.at[at], own.at[at], copy_sem.at[w]))
         loads[-1].start()
@@ -865,7 +1053,7 @@
     stores = []
 
     def wave_stages(w):
-        base, share, axis_order, _ = waves[w]
+        base, share, axis_order = waves[w]
         order = [name for name in axis_order if axes[name][1] > 1]
         state = {"at": base, "size": devices * share, "copies": [], "parts": []}
         taken = [base // 2]
@@ -975,11 +1163,10 @@
     depth = len(programs[0])
     for program in programs:
         program[0]()
-    last = max(wave[3] for wave in waves) + depth
-    for time in range(1, max(last, len(order) + 2)):
-        for w, wave in enumerate(waves):
-            if 1 <= time - wave[3] < depth:
-                programs[w][time - wave[3]]()
+    for time in range(1, max(depth, len(order) + 2)):
+        if time < depth:
+            for program in programs:
+                program[time]()
         if 1 <= time <= len(order) + 1:
             if time > 1:
                 small_end(order[time - 2])
@@ -1124,15 +1311,15 @@
         wide = widths[which]
         down_old, along_old = line_refs[which]
         down_out, along_out = line_outs[which]
-        down = jnp.broadcast_to(down_old[...], (LANE, columns)).T
+        down = jnp.broadcast_to(down_old[...].reshape(1, columns), (LANE, columns)).T
         down = decay_rate * down + (1.0 - decay_rate) * (
             row_s[which] * (factor * factor) / wide + FLOOR_ONE
         )
-        along = decay_rate * along_old[...] + (1.0 - decay_rate) * (
+        along = decay_rate * along_old[...].reshape(1, wide) + (1.0 - decay_rate) * (
             col_squares[which] * (factor * factor) / columns + FLOOR_ONE
         )
-        down_out[...] = down.T[:1, :]
-        along_out[...] = along
+        down_out[...] = down.T[:1, :].reshape(columns)
+        along_out[...] = along.reshape(wide)
         down = down[:, :1]
         if which == 3:
             along = along / (jnp.sum(along, axis=1, keepdims=True) / wide)
@@ -1195,8 +1382,7 @@
     head_count = vectors[3].shape[1]
     units = weights[2].shape[1]
     parts = units // columns
-    flat = lambda v: v.reshape(1, -1)
-    lines = [[flat(r), flat(c)] for r, c in zip(rows, cols)]
+    lines = [[r, c] for r, c in zip(rows, cols)]
     lines[3] = lines[3][::-1]
     vectors = [v.reshape(parts, columns) if v.ndim == 1 else v for v in vectors]
     moments = [v.reshape(parts, columns) if v.ndim == 1 else v for v in moments]
@@ -1239,7 +1425,7 @@
     norm, grads, news, vgrads, vnews, line_new, moment_new = made
     spread = lambda group: [v.reshape(-1) if i == 2 else v for i, v in enumerate(group)]
     line_new[3] = line_new[3][::-1]
-    moved = [line.reshape(-1) for pair in line_new for line in pair]
+    moved = [line for pair in line_new for line in pair]
     grads[3], news[3] = grads[3].T, news[3].T
     return (
         norm.reshape(1),
@@ -1361,7 +1547,7 @@
         1.0 - STEP ** (-0.8),
     )
     output, input_grad = unpack_images(
-        results, order, classes, band, chunks, inputs.shape[1]
+        results, order, classes, band, chunks, inputs.shape[1], columns
     )
     return (jnp.swapaxes(output, 0, 1), jnp.swapaxes(input_grad, 0, 1), *updated)
 

time: 315 us -> 303 us (0.962)
  Pallas kernels: 274 us -> 267 us
  other arithmetic: 7.92 us -> 4.04 us
    pallas_call x1, Pallas kernels: 71.2 us -> 60.1 us  [reduce_all(): pl.pallas_call(functools.partial(reduce_kernel, waves, rank_z), out_shape...]
    pallas_call x2, Pallas kernels: 131 us -> 137 us  [run_images(): pl.pallas_call(body, grid_spec=pltpu.PrefetchScalarGridSpec(num_scalar_pr...]
    pallas_call x3 -> x0, other arithmetic: 3.93 us -> none  [update_all(): pl.pallas_call(functools.partial(update_kernel, decay_rate, head_count, w...]
  transfers between devices with their start and end apart: 12 -> 12, of which waited for: 2 -> 2; matrix products, arithmetic and copies ran while one was open for 5% -> 3% of each run, Pallas kernels for 57% -> 61%
where the time goes in v2:
time: 303 us; the launch traced here: 298 us
  Pallas kernels  267 us (88%)
  starting transfers between devices  10.2 us (3%)
  local copies, waits for them, and re-layouts  8.8 us (3%)
  waiting for transfers between devices  6.38 us (2%)
  other arithmetic  4.04 us (1%)
    pallas_call x2, Pallas kernels, run_images(): pl.pallas_call(body, grid_spec=pltpu.PrefetchScalarGridSpec(num_scalar_pr...  137 us
    pallas_call x1, Pallas kernels, reduce_all(): pl.pallas_call(functools.partial(reduce_kernel, waves, rank_z), out_shape...  60.1 us
    pallas_call x1, Pallas kernels, update_all(): pl.pallas_call(functools.partial(update_kernel, decay_rate, head_count, w...  21.8 us
    pallas_call x2, Pallas kernels, pack_images(): pl.pallas_call(functools.partial(pack_kernel, first), grid_spec=pltpu.Pre...  17.9 us
    pallas_call x1, Pallas kernels, prepare(): pl.pallas_call(prep_kernel, out_shape=outs, in_specs=[smem, smem] + [vmem...  15.8 us
    pallas_call x1, Pallas kernels, unpack_images(): pl.pallas_call(functools.partial(unpack_kernel, chunks, bands), grid_spec...  15.3 us
    ppermute x12, starting transfers between devices, exchange(): lax.ppermute(parts[step], 'band', swaps[step])  10.2 us
    ppermute x12, waiting for transfers between devices, exchange(): lax.ppermute(parts[step], 'band', swaps[step])  6.38 us
  transfers between devices with their start and end apart: 12, of which 2 were waited for; matrix products, arithmetic and copies ran while one was open for 3% of the time, Pallas kernels for 61%

profile of v2, /device:TPU:0, one launch (start us, length us, event | category | flops | bytes accessed | tf_op | source)
XLA Modules:
  0.0 298.0 jit_solution(12978631793946570586)
XLA Ops:
  0.7 0.9 convert_reduce_fusion
  1.6 1.4 select_reduce_fusion
  3.0 0.5 fusion.2.class_ref
  3.5 9.0 %shard_map.725 = (bf16[2,4,112,384]{3,2,1,0:T(8,128)(2,1)}, bf16[2,4,112,384]{3,2,1,0:T(8,128)(2,1)}, bf16[2,4,112,384]{3,2,1,0:T(8,128)(2,1)}, bf16[2,4,112,384]{3,2,1,0:T(8,128)(2,1)}) custom-call(s32[32]{0:T(128)} %get-tuple-element.206.order_ref, s32[32]{0:T(128)} %fusion.2.class_ref, s32[1]{0:T(128)} %bitcast.band_ref, bf16[100,32,432]{2,1,0:T(8,128)(2,1)} %bitcast.12, ...), custom_call_target="tpu_custom_call" | custom-call | flops 10000000 | bytes 10000000 | tf_op jit(solution)/shard_map/pallas_call | solution.py:768
  12.5 0.5 collective-permute-start
  13.0 2.6 collective-permute-start.1
  15.6 0.1 collective-permute-start.2
  15.7 0.1 dynamic_slice.3
  15.8 0.0 copy-done.5
  15.8 0.6 pad.4.fc1b_ref
  16.4 8.9 %shard_map.723 = (bf16[2,4,112,384]{3,2,1,0:T(8,128)(2,1)}, bf16[2,4,112,384]{3,2,1,0:T(8,128)(2,1)}, bf16[2,4,112,384]{3,2,1,0:T(8,128)(2,1)}, bf16[2,4,112,384]{3,2,1,0:T(8,128)(2,1)}) custom-call(s32[32]{0:T(128)} %get-tuple-element.206.order_ref, s32[32]{0:T(128)} %fusion.2.class_ref, s32[1]{0:T(128)} %bitcast.band_ref, bf16[100,32,432]{2,1,0:T(8,128)(2,1)} %bitcast.13, ...), custom_call_target="tpu_custom_call" | custom-call | flops 10000000 | bytes 10000000 | tf_op jit(solution)/shard_map/pallas_call | solution.py:768
  25.3 1.2 broadcast_subtract_fusion
  26.5 15.8 %shard_map.724 = (bf16[432,1536]{1,0:T(8,128)(2,1)}, bf16[432,1296]{1,0:T(8,128)(2,1)}, bf16[512,432]{1,0:T(8,128)(2,1)}, bf16[432,1792]{1,0:T(8,128)(2,1)}, bf1...) custom-call(f32[4,9]{1,0:T(4,128)} %vector_refs_3_.1, ...), custom_call_target="tpu_custom_call" | custom-call | flops 50000000 | bytes 22000000 | tf_op jit(solution)/shard_map/pallas_call | solution.py:934
  42.3 0.6 fusion.4
  42.9 0.0 collective-permute-done.xct_refs_1_
  42.9 0.0 collective-permute-done.1.xct_refs_2_
  42.9 0.0 copy-start.9
  42.9 3.5 %collective-permute-done.2.xct_refs_3_ = bf16[2,4,112,384]{3,2,1,0:T(8,128)(2,1)S(1)} collective-permute-done((bf16[2,4,112,384]{3,2,1,0:T(8,128)(2,1)}, bf16[2,4,112,384]{3,2,1,0:T(8,128)(2,1)S(1)}, u32[]{:S(2)}, u32[]{:S(2)}) %collective-permute-start.2) | collective-permute-done | bytes 688160 | tf_op jit(solution)/shard_map/ppermute | solution.py:1506
  46.3 0.1 collective-permute-start.6
  46.5 1.7 collective-permute-start.7
  48.2 0.0 copy-done.8
  48.2 0.0 collective-permute-start.8
  48.2 0.6 broadcast_in_dim.42.tiles_in
  48.8 0.6 broadcast_in_dim.43.small_in
  49.4 0.0 copy-done.7
  49.4 0.0 copy-done.9
  49.4 0.0 copy-done.11
  49.4 87.6 %shard_map.726 = (bf16[2,4,112,384]{3,2,1,0:T(8,128)(2,1)}, bf16[2,4,112,384]{3,2,1,0:T(8,128)(2,1)}, bf16[2,4,112,384]{3,2,1,0:T(8,128)(2,1)}, bf16[2,4,112,384...) custom-call(s32[4]{0:T(128)} %get-tuple-element.210.sizes_ref, s32[1]{0:T(128)} %bitcast.band_ref, ...), custom_call_target="tpu_custom_call" | custom-call | flops 32000000000 | bytes 40000000 | tf_op jit(solution)/shard_map/pallas_call | solution.py:681
  137.0 1.5 collective-permute-start.3
  138.5 1.7 collective-permute-start.4
  140.2 0.0 collective-permute-done.6.xct_refs_1_
  140.2 0.0 collective-permute-start.5
  140.2 0.0 collective-permute-done.7.xct_refs_2_
  140.2 0.0 collective-permute-done.8.xct_refs_3_
  140.2 0.8 copy-done.10
  141.1 49.0 %shard_map.727 = (bf16[2,4,112,384]{3,2,1,0:T(8,128)(2,1)}, bf16[2,4,112,384]{3,2,1,0:T(8,128)(2,1)}, bf16[2,4,112,384]{3,2,1,0:T(8,128)(2,1)}, bf16[2,4,112,384...) custom-call(s32[4]{0:T(128)} %get-tuple-element.209.sizes_ref, s32[1]{0:T(128)} %bitcast.band_ref, ...), custom_call_target="tpu_custom_call" | custom-call | flops 32000000000 | bytes 40000000 | tf_op jit(solution)/shard_map/pallas_call | solution.py:681
  190.1 0.0 copy-start.6
  190.1 0.0 collective-permute-done.3.refs_1_
  190.1 0.0 copy-start
  190.1 0.0 collective-permute-done.4.refs_2_
  190.1 0.0 copy-start.1
  190.2 0.0 collective-permute-done.5.refs_3_
  190.2 0.0 copy-start.2
  190.2 60.1 %shard_map.728 = (bf16[1184,16,128]{2,1,0:T(8,128)(2,1)}, f32[16,512]{1,0:T(8,128)}) custom-call(bf16[1184,16,128]{2,1,0:T(8,128)(2,1)} %get-tuple-element.165.own_ref, f32[16,512]{1,0:T(8,128)} %get-tuple-element.166.small_ref), custom_call_target="tpu_custom_call" | custom-call | flops 10000000 | bytes 200000000 | tf_op jit(solution)/shard_map/pallas_call | solution.py:1185
  250.3 0.4 collective-permute-start.9
  250.7 0.3 collective-permute-start.10
  251.0 1.2 collective-permute-start.11
  252.2 0.7 reshape.136.vector_refs_2_
  252.9 0.0 copy-done.6
  252.9 0.7 reshape.137.moment_refs_2_
  253.6 21.8 %shard_map.730 = (f32[1,1]{1,0:T(1,128)}, f32[432,1296]{1,0:T(8,128)}, f32[432,432]{1,0:T(8,128)}, f32[432,1728]{1,0:T(8,128)}, f32[432,1728]{1,0:T(8,128)}, /*i...) custom-call(bf16[1184,16,128]{2,1,0:T(8,128)(2,1)} %get-tuple-elemen, ...), custom_call_target="tpu_custom_call" | custom-call | tf_op jit(solution)/shard_map/pallas_call | solution.py:1417
  275.4 0.0 copy-done
  275.4 0.0 copy-done.1
  275.4 0.0 copy-done.2
  275.4 1.4 reshape.139
  276.8 1.4 reshape.140
  278.2 1.4 reshape.141
  279.5 0.0 collective-permute-done.9.refs_5_
  279.5 0.0 collective-permute-done.10.refs_6_
  279.5 0.0 copy-start.4
  279.6 2.9 collective-permute-done.11.refs_7_
  282.4 0.0 copy-done.3
  282.4 0.0 copy-done.4
  282.4 15.3 %shard_map.729 = (bf16[100,32,432]{2,1,0:T(8,128)(2,1)}, f32[100,32,432]{2,1,0:T(8,128)}) custom-call(s32[32]{0:T(128)} %get-tuple-element.206.order_ref, s32[32]{0:T(128)} %fusion.2.class_ref, s32[1]{0:T(128)} %bitcast.band_ref, bf16[3,100,96]{2,1,0:T(8,128)(2,1)} %constant.107.clone.table_ref, bf16[3,100,48]{2,1,0:T(8,128)(2,1)} %constant.108.clone.low_ref, ...), custom_call_target="tpu_custom_call" | custom-call | flops 10000000 | bytes 16000000 | tf_op jit(solution)/shard_map/pallas_call | solution.py:846
  (8 shorter events, 0.0 us)
Async XLA Ops:
  3.5 12.3 %copy-start.5 = (f32[1728]{0:T(1024)S(1)}, f32[1728]{0:T(1024)}, u32[]{:S(2)}) copy-start(f32[1728]{0:T(1024)} %param.61) | copy-start | bytes 20740
  12.5 30.3 %collective-permute-start = (bf16[2,4,112,384]{3,2,1,0:T(8,128)(2,1)}, bf16[2,4,112,384]{3,2,1,0:T(8,128)(2,1)S(1)}, u32[]{:S(2)}, u32[]{:S(2)}) collective-permute-start(bf16[2,4,112,384]{3,2,1,0:T(8,128)(2,1)} %get-tuple-element.128), channel_id=1, source_target_pairs={{0,1},{1,0},{2,3},{3,2},{4,5},{5,4},{6,7},{7,6},{8,9},{9,8},{10,11... | collective-permute-start | bytes 2064392 | tf_op jit(solution)/shard_map/ppermute | solution.py:1506
  13.0 29.8 %collective-permute-start.1 = (bf16[2,4,112,384]{3,2,1,0:T(8,128)(2,1)}, bf16[2,4,112,384]{3,2,1,0:T(8,128)(2,1)S(1)}, u32[]{:S(2)}, u32[]{:S(2)}) collective-permute-start(bf16[2,4,112,384]{3,2,1,0:T(8,128)(2,1)} %get-tuple-element.129), channel_id=1, source_target_pairs={{0,2},{1,3},{2,0},{3,1},{4,6},{5,7},{6,4},{7,5},{8,10},{9,11},{10,... | collective-permute-start | bytes 2064392 | tf_op jit(solution)/shard_map/ppermute | solution.py:1506
  15.6 30.7 %collective-permute-start.2 = (bf16[2,4,112,384]{3,2,1,0:T(8,128)(2,1)}, bf16[2,4,112,384]{3,2,1,0:T(8,128)(2,1)S(1)}, u32[]{:S(2)}, u32[]{:S(2)}) collective-permute-start(bf16[2,4,112,384]{3,2,1,0:T(8,128)(2,1)} %get-tuple-element.130), channel_id=1, source_target_pairs={{0,3},{1,2},{2,1},{3,0},{4,7},{5,6},{6,5},{7,4},{8,11},{9,10},{10,... | collective-permute-start | bytes 2064392 | tf_op jit(solution)/shard_map/ppermute | solution.py:1506
  26.5 21.7 %copy-start.8 = (bf16[2,4,112,384]{3,2,1,0:T(8,128)(2,1)S(1)}, bf16[2,4,112,384]{3,2,1,0:T(8,128)(2,1)}, u32[]{:S(2)}) copy-start(bf16[2,4,112,384]{3,2,1,0:T(8,128)(2,1)} %get-tuple-element.153) | copy-start | bytes 2064388
  42.9 6.6 %copy-start.7 = (bf16[2,4,112,384]{3,2,1,0:T(8,128)(2,1)}, bf16[2,4,112,384]{3,2,1,0:T(8,128)(2,1)S(1)}, u32[]{:S(2)}) copy-start(bf16[2,4,112,384]{3,2,1,0:T(8,128)(2,1)S(1)} %collective-permute-done.xct_refs_1_) | copy-start | bytes 2064388
  42.9 6.5 %copy-start.9 = (bf16[2,4,112,384]{3,2,1,0:T(8,128)(2,1)}, bf16[2,4,112,384]{3,2,1,0:T(8,128)(2,1)S(1)}, u32[]{:S(2)}) copy-start(bf16[2,4,112,384]{3,2,1,0:T(8,128)(2,1)S(1)} %collective-permute-done.1.xct_refs_2_) | copy-start | bytes 2064388
  46.3 3.1 %copy-start.11 = (bf16[2,4,112,384]{3,2,1,0:T(8,128)(2,1)}, bf16[2,4,112,384]{3,2,1,0:T(8,128)(2,1)S(1)}, u32[]{:S(2)}) copy-start(bf16[2,4,112,384]{3,2,1,0:T(8,128)(2,1)S(1)} %collective-permute-done.2.xct_refs_3_) | copy-start | bytes 2064388
  46.3 93.9 %collective-permute-start.6 = (bf16[2,4,112,384]{3,2,1,0:T(8,128)(2,1)}, bf16[2,4,112,384]{3,2,1,0:T(8,128)(2,1)S(1)}, u32[]{:S(2)}, u32[]{:S(2)}) collective-permute-start(bf16[2,4,112,384]{3,2,1,0:T(8,128)(2,1)} %get-tuple-element.151), channel_id=1, source_target_pairs={{0,1},{1,0},{2,3},{3,2},{4,5},{5,4},{6,7},{7,6},{8,9},{9,8},{10,11... | collective-permute-start | bytes 2064392 | tf_op jit(solution)/shard_map/ppermute | solution.py:1506
  46.5 93.8 %collective-permute-start.7 = (bf16[2,4,112,384]{3,2,1,0:T(8,128)(2,1)}, bf16[2,4,112,384]{3,2,1,0:T(8,128)(2,1)}, u32[]{:S(2)}, u32[]{:S(2)}) collective-permute-start(bf16[2,4,112,384]{3,2,1,0:T(8,128)(2,1)} %get-tuple-element.152), channel_id=1, source_target_pairs={{0,2},{1,3},{2,0},{3,1},{4,6},{5,7},{6,4},{7,5},{8,10},{9,11},{10,... | collective-permute-start | bytes 2064392 | tf_op jit(solution)/shard_map/ppermute | solution.py:1506
  48.2 92.1 %collective-permute-start.8 = (bf16[2,4,112,384]{3,2,1,0:T(8,128)(2,1)S(1)}, bf16[2,4,112,384]{3,2,1,0:T(8,128)(2,1)}, u32[]{:S(2)}, u32[]{:S(2)}) collective-permute-start(bf16[2,4,112,384]{3,2,1,0:T(8,128)(2,1)S(1)} %copy-done.8), channel_id=1, source_target_pairs={{0,3},{1,2},{2,1},{3,0},{4,7},{5,6},{6,5},{7,4},{8,11},{9,10},{10,... | collective-permute-start | bytes 2064392 | tf_op jit(solution)/shard_map/ppermute | solution.py:1506
  137.0 53.1 %collective-permute-start.3 = (bf16[2,4,112,384]{3,2,1,0:T(8,128)(2,1)}, bf16[2,4,112,384]{3,2,1,0:T(8,128)(2,1)S(1)}, u32[]{:S(2)}, u32[]{:S(2)}) collective-permute-start(bf16[2,4,112,384]{3,2,1,0:T(8,128)(2,1)} %get-tuple-element.147), channel_id=1, source_target_pairs={{0,1},{1,0},{2,3},{3,2},{4,5},{5,4},{6,7},{7,6},{8,9},{9,8},{10,11... | collective-permute-start | bytes 2064392 | tf_op jit(solution)/shard_map/ppermute | solution.py:1506
  138.5 51.6 %collective-permute-start.4 = (bf16[2,4,112,384]{3,2,1,0:T(8,128)(2,1)}, bf16[2,4,112,384]{3,2,1,0:T(8,128)(2,1)S(1)}, u32[]{:S(2)}, u32[]{:S(2)}) collective-permute-start(bf16[2,4,112,384]{3,2,1,0:T(8,128)(2,1)} %get-tuple-element.148), channel_id=1, source_target_pairs={{0,2},{1,3},{2,0},{3,1},{4,6},{5,7},{6,4},{7,5},{8,10},{9,11},{10,... | collective-permute-start | bytes 2064392 | tf_op jit(solution)/shard_map/ppermute | solution.py:1506
  140.2 0.8 copy-start.10
  140.2 49.9 %collective-permute-start.5 = (bf16[2,4,112,384]{3,2,1,0:T(8,128)(2,1)}, bf16[2,4,112,384]{3,2,1,0:T(8,128)(2,1)S(1)}, u32[]{:S(2)}, u32[]{:S(2)}) collective-permute-start(bf16[2,4,112,384]{3,2,1,0:T(8,128)(2,1)} %get-tuple-element.149), channel_id=1, source_target_pairs={{0,3},{1,2},{2,1},{3,0},{4,7},{5,6},{6,5},{7,4},{8,11},{9,10},{10,... | collective-permute-start | bytes 2064392 | tf_op jit(solution)/shard_map/ppermute | solution.py:1506
  190.1 62.8 %copy-start.6 = (f32[1728]{0:T(1024)S(1)}, f32[1728]{0:T(1024)}, u32[]{:S(2)}) copy-start(f32[1728]{0:T(1024)} %param.73) | copy-start | bytes 20740
  190.1 85.3 %copy-start = (bf16[2,4,112,384]{3,2,1,0:T(8,128)(2,1)}, bf16[2,4,112,384]{3,2,1,0:T(8,128)(2,1)S(1)}, u32[]{:S(2)}) copy-start(bf16[2,4,112,384]{3,2,1,0:T(8,128)(2,1)S(1)} %collective-permute-done.3.refs_1_) | copy-start | bytes 2064388
  190.1 85.2 %copy-start.1 = (bf16[2,4,112,384]{3,2,1,0:T(8,128)(2,1)}, bf16[2,4,112,384]{3,2,1,0:T(8,128)(2,1)S(1)}, u32[]{:S(2)}) copy-start(bf16[2,4,112,384]{3,2,1,0:T(8,128)(2,1)S(1)} %collective-permute-done.4.refs_2_) | copy-start | bytes 2064388
  190.2 85.2 %copy-start.2 = (bf16[2,4,112,384]{3,2,1,0:T(8,128)(2,1)}, bf16[2,4,112,384]{3,2,1,0:T(8,128)(2,1)S(1)}, u32[]{:S(2)}) copy-start(bf16[2,4,112,384]{3,2,1,0:T(8,128)(2,1)S(1)} %collective-permute-done.5.refs_3_) | copy-start | bytes 2064388
  250.3 29.3 %collective-permute-start.9 = (bf16[2,4,112,384]{3,2,1,0:T(8,128)(2,1)}, bf16[2,4,112,384]{3,2,1,0:T(8,128)(2,1)S(1)}, u32[]{:S(2)}, u32[]{:S(2)}) collective-permute-start(bf16[2,4,112,384]{3,2,1,0:T(8,128)(2,1)} %get-tuple-element.169), channel_id=1, source_target_pairs={{0,1},{1,0},{2,3},{3,2},{4,5},{5,4},{6,7},{7,6},{8,9},{9,8},{10,11... | collective-permute-start | bytes 2064392 | tf_op jit(solution)/shard_map/ppermute | solution.py:1506
  250.7 28.8 %collective-permute-start.10 = (bf16[2,4,112,384]{3,2,1,0:T(8,128)(2,1)}, bf16[2,4,112,384]{3,2,1,0:T(8,128)(2,1)S(1)}, u32[]{:S(2)}, u32[]{:S(2)}) collective-permute-start(bf16[2,4,112,384]{3,2,1,0:T(8,128)(2,1)} %get-tuple-element.170), channel_id=1, source_target_pairs={{0,2},{1,3},{2,0},{3,1},{4,6},{5,7},{6,4},{7,5},{8,10},{9,11},{10,... | collective-permute-start | bytes 2064392 | tf_op jit(solution)/shard_map/ppermute | solution.py:1506
  251.0 31.4 %collective-permute-start.11 = (bf16[2,4,112,384]{3,2,1,0:T(8,128)(2,1)}, bf16[2,4,112,384]{3,2,1,0:T(8,128)(2,1)}, u32[]{:S(2)}, u32[]{:S(2)}) collective-permute-start(bf16[2,4,112,384]{3,2,1,0:T(8,128)(2,1)} %get-tuple-element.171), channel_id=1, source_target_pairs={{0,3},{1,2},{2,1},{3,0},{4,7},{5,6},{6,5},{7,4},{8,11},{9,10},{10,... | collective-permute-start | bytes 2064392 | tf_op jit(solution)/shard_map/ppermute | solution.py:1506
  279.5 2.9 copy-start.3
  279.5 2.9 copy-start.4
